TPU v7x, 128 devices: a whole 4x4x4 slice. The times are simulated.
128 devices in a mesh: coarse: 4 (over z_hi, core), leaf: 32 (over x, y, z_lo).
Axes of the slice: x: 4, y: 4, z: 4 (z_hi: 2, z_lo: 2; z = z_hi * 2 + z_lo), core: 2. Of those that a mesh axis runs over, the one named last changes fastest.
Arguments:
- densities: bfloat16 [65536, 128], P(('coarse', 'leaf')), may hold values from -6 to 6
- cotangents: bfloat16 [65536, 128], P(('coarse', 'leaf')), may hold values from -6 to 6
- far_list: int32 [16, 65536], P(None, ('coarse', 'leaf')), may hold values from -1 to 256, as said below
- near_list: int32 [27, 65536], P(None, ('coarse', 'leaf')), may hold values from -1 to 256, as said below
- coarse_list: int32 [16, 16], replicated, may hold values from -1 to 15, as said below
- to_moments: bfloat16 [128, 256], replicated, may hold values from -0.5 to 0.5
- merge_moments: bfloat16 [8, 256, 256], replicated, may hold values from -0.125 to 0.125
- far_translate: bfloat16 [16, 256, 256], replicated, may hold values from -0.09375 to 0.09375
- local_split: bfloat16 [256, 8, 256], replicated, may hold values from -0.375 to 0.375
- to_values: bfloat16 [256, 128], replicated, may hold values from -0.375 to 0.375
- near_blocks: bfloat16 [27, 128, 128], replicated, may hold values from -0.109375 to 0.109375
Outputs:
- potential: float32 [65536, 128], P(('coarse', 'leaf'))
- gradient: float32 [65536, 128], P(('coarse', 'leaf'))
Inputs may be any that keep to these rules, and one draw needn't show every extreme that they name: `far_list`: -1 marks an empty slot; any other entry e of box b names the leaf box b + e - 128, which exists. `near_list`: -1 marks an empty slot; any other entry e of box b names the leaf box b + e - 128, which exists. `coarse_list`: -1 marks an empty slot; any other entry is a box of the coarse level.
All inputs are finite; a program needn't handle non-finite values.
Results may differ from a plain program's by a relative error of at most 0.018.
Values may be sent and summed in bfloat16 or wider, within the bound.
No kernel may reach another device: no remote copies, remote signals or barrier semaphores. Data moves between devices by JAX's collectives and lax.ppermute only.
A program may use at most 128 MiB of HBM per device.

v0:
```python
import functools

import jax
import jax.numpy as jnp
from jax import lax
from jax.experimental import pallas as pl
from jax.experimental.pallas import tpu as pltpu
from jax.sharding import PartitionSpec as P

HW = 128
TILE = 256
AXES = ("coarse", "leaf")
F32 = jnp.float32
BF16 = jnp.bfloat16
NN = (((1,), (0,)), ((), ()))
NT = (((1,), (1,)), ((), ()))


def dot(a, b, dims=NN):
    return lax.dot_general(a, b, dims, preferred_element_type=F32)


def rounded(x):
    return x.astype(BF16).astype(F32)


def whole(count):
    return [pl.BlockSpec(memory_space=pltpu.VMEM)] * count


def get_rows(ref, at):
    return jnp.concatenate([ref[h, at, :] for h in range(ref.shape[0])], axis=1)


def put_rows(ref, at, x):
    for h in range(ref.shape[0]):
        ref[h, at, :] = x[:, h * 128 : (h + 1) * 128]


def climb_kernel(dens, cot, to_m, to_v, merge, split, out, mom, adj):
    rows = dens.shape[0]
    k = to_m.shape[1]
    put_rows(mom, pl.ds(0, rows), rounded(dot(dens[...], to_m[...])))
    put_rows(adj, pl.ds(0, rows), rounded(dot(cot[...], to_v[...], NT)))
    while rows > 1:
        rows //= 8
        up = jnp.zeros((rows, k), F32)
        adj_up = jnp.zeros((rows, k), F32)
        for c in range(8):
            child = pl.ds(c, rows, stride=8) if rows > 1 else pl.ds(c, 1)
            up += dot(get_rows(mom, child).astype(BF16), merge[c])
            adj_up += dot(get_rows(adj, child).astype(BF16), split[:, c * k : (c + 1) * k], NT)
        put_rows(mom, pl.ds(0, rows), rounded(up))
        put_rows(adj, pl.ds(0, rows), rounded(adj_up))
    row = jnp.concatenate([mom[0, :1], mom[1, :1], adj[0, :1], adj[1, :1], jnp.zeros((4, 128), F32)], axis=0)
    out[...] = jnp.broadcast_to(row[None], (out.shape[0] // 8, 8, 128)).reshape(out.shape)


def near_far_kernel(
    place, far, near, dens, cot, recv_e, recv_o, to_m, to_v, far_w, near_w,
    leaf_far, near_val, adj_far, near_adj,
    dens_wide, cot_wide, mom_wide, adj_wide, row_targets, col_targets,
):
    rows = dens.shape[0]
    wide = rows + 2 * HW
    n_far, n_near = far.shape[0], near.shape[0]
    slots = n_far + n_near
    odd = lax.rem(place[0], 2) == 1
    first, second = recv_e[...], recv_o[...]
    left = jnp.where(odd, first, second)
    right = jnp.where(odd, second, first)
    for target, own, start in ((dens_wide, dens, 0), (cot_wide, cot, HW)):
        target[:HW, :] = left[start : start + HW]
        target[HW : HW + rows, :] = own[...]
        target[HW + rows :, :] = right[start : start + HW]
    mom_wide[...] = dot(dens_wide[...], to_m[...]).astype(BF16)
    adj_wide[...] = dot(cot_wide[...], to_v[...], NT).astype(BF16)

    padded = row_targets.shape[0]
    row_targets[...] = jnp.full(row_targets.shape, -1.0, F32)
    row_targets[:, :HW] = left[2 * HW :].astype(F32)
    row_targets[:n_far, HW : HW + rows] = far[...].astype(F32)
    row_targets[n_far:slots, HW : HW + rows] = near[...].astype(F32)
    row_targets[:, HW + rows :] = right[2 * HW :].astype(F32)
    own = row_targets[:, HW : HW + rows]
    own = jnp.concatenate([own, jnp.full((128 - padded, rows), -1.0, F32)], axis=0)
    own = own.T
    place_r = (lax.broadcasted_iota(jnp.int32, own.shape, 0) % TILE).astype(F32)
    col_targets[...] = jnp.where(own >= 0, own + place_r, -1.0)
    entries = row_targets[...]
    place_w = (lax.broadcasted_iota(jnp.int32, entries.shape, 1) % TILE).astype(F32)
    row_targets[...] = jnp.where(entries >= 0, entries + place_w, -1.0)

    leaf_far[...] = jnp.zeros(leaf_far.shape, F32)
    near_val[...] = jnp.zeros(near_val.shape, F32)
    adj_far[...] = jnp.zeros(adj_far.shape, F32)
    near_adj[...] = jnp.zeros(near_adj.shape, F32)
    lane = lax.broadcasted_iota(jnp.int32, (TILE, 128), 1).astype(F32)
    lanes = [lane.astype(BF16), (lane + 128.0).astype(BF16)]
    down = lax.broadcasted_iota(jnp.int32, (TILE, TILE), 0).astype(F32).astype(BF16)
    one = jnp.ones((), BF16)
    zero = jnp.zeros((), BF16)

    def step(slot, operator, fwd_src, fwd_out, adj_src, adj_out):
        for p in range(rows // TILE):
            own = pl.ds(p * TILE, TILE)
            reach = pl.ds(p * TILE, 2 * TILE)
            column = col_targets[own, :]
            column = jnp.take_along_axis(column, jnp.full(column.shape, slot, jnp.int32), axis=1)
            low, high = column.astype(BF16), (column - TILE).astype(BF16)
            table = jnp.concatenate(
                [jnp.where(c == t, one, zero) for t in (low, high) for c in lanes], axis=1
            )
            picked = dot(table, fwd_src[reach, :]).astype(BF16)
            fwd_out[own, :] += dot(picked, operator)
            entry = row_targets[pl.ds(slot, 1), p * TILE : (p + 2) * TILE]
            high = jnp.broadcast_to(entry[:, :TILE] - TILE, (TILE, TILE)).astype(BF16)
            low = jnp.broadcast_to(entry[:, TILE:], (TILE, TILE)).astype(BF16)
            table = jnp.concatenate(
                [jnp.where(down == t, one, zero) for t in (high, low)], axis=1
            )
            collected = dot(table, adj_src[reach, :]).astype(BF16)
            adj_out[own, :] += dot(collected, operator, NT)

    @pl.loop(0, n_far)
    def _(j):
        step(j, far_w[j], mom_wide, leaf_far, adj_wide, adj_far)

    @pl.loop(0, n_near)
    def _(j):
        step(j + n_far, near_w[j], dens_wide, near_val, cot_wide, near_adj)


def fall_kernel(
    place, gathered, coarse_list, coarse_list_t, merge, far_w, split, to_m, to_v,
    leaf_far, near_val, adj_far, near_adj,
    potential, gradient,
    fall, adj_fall,
):
    k = merge.shape[2]
    boxes = coarse_list.shape[1]
    coarse_m = jnp.zeros((boxes, k), F32)
    coarse_a = jnp.zeros((boxes, k), F32)
    for c in range(8):
        parts = [gathered[pl.ds(8 * c + i, boxes, stride=64), :] for i in range(4)]
        moments = jnp.concatenate(parts[:2], axis=1).astype(BF16)
        adjoints = jnp.concatenate(parts[2:], axis=1).astype(BF16)
        coarse_m += dot(moments, merge[c])
        coarse_a += dot(adjoints, split[:, c * k : (c + 1) * k], NT)
    coarse_m = coarse_m.astype(BF16)
    coarse_a = coarse_a.astype(BF16)
    local = jnp.zeros((boxes, k), F32)
    adjoint = jnp.zeros((boxes, k), F32)
    across = lax.broadcasted_iota(jnp.int32, (boxes, boxes), 1)
    along = lax.broadcasted_iota(jnp.int32, (boxes, boxes), 0)
    for j in range(far_w.shape[0]):
        table = jnp.where(across == coarse_list_t[:, j : j + 1], 1.0, 0.0).astype(BF16)
        local += dot(dot(table, coarse_m).astype(BF16), far_w[j])
        table = jnp.where(along == coarse_list[j : j + 1, :], 1.0, 0.0).astype(BF16)
        adjoint += dot(dot(table, coarse_a).astype(BF16), far_w[j], NT)
    put_rows(fall, pl.ds(0, boxes), rounded(local))
    put_rows(adj_fall, pl.ds(0, boxes), rounded(adjoint))
    box, child = place[0] // 8, lax.rem(place[0], 8)
    top = get_rows(fall, pl.ds(box, 1)).astype(BF16)
    adj_top = get_rows(adj_fall, pl.ds(box, 1)).astype(BF16)
    put_rows(fall, pl.ds(0, 1), rounded(dot(top, split[:, pl.ds(pl.multiple_of(child * k, k), k)])))
    put_rows(adj_fall, pl.ds(0, 1), rounded(dot(adj_top, merge[child], NT)))
    rows = 1
    while rows < fall.shape[1]:
        parents = get_rows(fall, pl.ds(0, rows)).astype(BF16)
        adj_parents = get_rows(adj_fall, pl.ds(0, rows)).astype(BF16)
        for c in range(8):
            children = pl.ds(c, rows, stride=8) if rows > 1 else pl.ds(c, 1)
            put_rows(fall, children, rounded(dot(parents, split[:, c * k : (c + 1) * k])))
            put_rows(adj_fall, children, rounded(dot(adj_parents, merge[c], NT)))
        rows *= 8
    potential[...] = dot((leaf_far[...] + get_rows(fall, pl.ds(0, rows))).astype(BF16), to_v[...]) + near_val[...]
    gradient[...] = dot((adj_far[...] + get_rows(adj_fall, pl.ds(0, rows))).astype(BF16), to_m[...], NT) + near_adj[...]


def edge(odd, densities, cotangents, lists):
    rows = densities.shape[0]
    at = jnp.where(odd, rows - HW, 0)
    return jnp.concatenate(
        [
            lax.dynamic_slice_in_dim(densities, at, HW, 0),
            lax.dynamic_slice_in_dim(cotangents, at, HW, 0),
            lax.dynamic_slice_in_dim(lists, at, HW, 1),
        ],
        axis=0,
    )


def per_device(
    densities, cotangents, far_list, near_list, coarse_list,
    to_moments, merge_moments, far_translate, local_split, to_values, near_blocks,
):
    rows = densities.shape[0]
    k = to_moments.shape[1]
    count = lax.axis_size(AXES)
    here = lax.axis_index(AXES)
    place = here.astype(jnp.int32).reshape(1)
    odd = lax.rem(here, 2) == 1
    slots = far_list.shape[0] + near_list.shape[0]
    padded = -(-slots // 16) * 16
    lists = jnp.concatenate(
        [far_list, near_list, jnp.full((padded - slots, rows), -1, jnp.int32)], axis=0
    ).astype(BF16)
    recv_e = lax.ppermute(
        edge(~odd, densities, cotangents, lists), AXES, [(i, i ^ 1) for i in range(count)]
    )
    pairs = [(i, i + 1) for i in range(1, count - 1, 2)]
    recv_o = lax.ppermute(
        edge(odd, densities, cotangents, lists), AXES, pairs + [(b, a) for a, b in pairs]
    )
    split = local_split.reshape(k, 8 * k)
    smem = pl.BlockSpec(memory_space=pltpu.SMEM)

    row = pl.pallas_call(
        climb_kernel,
        out_shape=jax.ShapeDtypeStruct((count * 8, 128), F32),
        in_specs=whole(6),
        out_specs=pl.BlockSpec(memory_space=pltpu.VMEM),
        scratch_shapes=[pltpu.VMEM((k // 128, rows, 128), F32)] * 2,
        compiler_params=pltpu.CompilerParams(vmem_limit_bytes=16 << 20),
        name="climb",
    )(densities, cotangents, to_moments, to_values, merge_moments, split)
    gathered = lax.all_to_all(row, AXES, 0, 0, tiled=True)

    wide = rows + 2 * HW
    sums = pl.pallas_call(
        near_far_kernel,
        out_shape=[
            jax.ShapeDtypeStruct((rows, k), F32),
            jax.ShapeDtypeStruct((rows, 128), F32),
            jax.ShapeDtypeStruct((rows, k), F32),
            jax.ShapeDtypeStruct((rows, 128), F32),
        ],
        in_specs=[smem] + whole(10),
        out_specs=whole(4),
        scratch_shapes=[
            pltpu.VMEM((wide, 128), BF16),
            pltpu.VMEM((wide, 128), BF16),
            pltpu.VMEM((wide, k), BF16),
            pltpu.VMEM((wide, k), BF16),
            pltpu.VMEM((padded, wide), F32),
            pltpu.VMEM((rows, 128), F32),
        ],
        compiler_params=pltpu.CompilerParams(vmem_limit_bytes=40 << 20),
        cost_estimate=pl.CostEstimate(flops=20 * 10**9, bytes_accessed=5 << 20, transcendentals=0),
        name="near_far",
    )(
        place, far_list, near_list, densities, cotangents, recv_e, recv_o,
        to_moments, to_values, far_translate, near_blocks,
    )

    return pl.pallas_call(
        fall_kernel,
        out_shape=[jax.ShapeDtypeStruct((rows, 128), F32)] * 2,
        in_specs=[smem] + whole(12),
        out_specs=whole(2),
        scratch_shapes=[pltpu.VMEM((k // 128, rows, 128), F32)] * 2,
        compiler_params=pltpu.CompilerParams(vmem_limit_bytes=24 << 20),
        name="fall",
    )(
        place, gathered, coarse_list, coarse_list.T, merge_moments, far_translate, split,
        to_moments, to_values, *sums,
    )


def solution(mesh):
    rows = P(AXES, None)
    lists = P(None, AXES)
    return jax.shard_map(
        per_device,
        mesh=mesh,
        in_specs=(rows, rows, lists, lists) + (P(),) * 7,
        out_specs=(rows, rows),
        check_vma=False,
    )
```

profile of v0, /device:TPU:1, one launch (start us, length us, event | category | flops | bytes accessed | tf_op | source)
XLA Modules:
  0.0 91.2 jit_solution(7158094203376839397)
XLA Ops:
  0.6 0.0 copy-start.6
  0.6 0.0 copy-start.5
  0.7 0.0 copy-start.8
  0.7 0.0 copy-start.7
  0.7 0.0 copy-start
  0.7 0.9 convert.8
  1.6 0.8 convert.9
  2.4 0.1 pad.8.clone
  2.5 0.1 maximum_maximum_fusion
  2.6 0.8 constant_dynamic-slice_fusion.1
  3.4 2.5 %collective-permute-start = (bf16[304,128]{1,0:T(8,128)(2,1)S(1)}, bf16[304,128]{1,0:T(8,128)(2,1)S(1)}, u32[]{:S(2)}, u32[]{:S(2)}) collective-permute-start(bf16[304,128]{1,0:T(8,128)(2,1)S(1)} %pad_maximum_fusion), channel_id=1, source_target_pairs={{0,1},{1,0},{2,3},{3,2},{4,5},{5,4},{6,7},{7,6},{8,9},{9,8},{10,11... | collective-permute-start | bytes 233480 | tf_op jit(solution)/shard_map/ppermute | solution.py:209
  6.0 7.2 %collective-permute-start.1 = (bf16[304,128]{1,0:T(8,128)(2,1)S(1)}, bf16[304,128]{1,0:T(8,128)(2,1)S(1)}, u32[]{:S(2)}, u32[]{:S(2)}) collective-permute-start(bf16[304,128]{1,0:T(8,128)(2,1)S(1)} %pad_maximum_fusion.1), channel_id=1, source_target_pairs={{1,2},{3,4},{5,6},{7,8},{9,10},{11,12},{13,14},{15,16},{17,18},{19... | collective-permute-start | bytes 233480 | tf_op jit(solution)/shard_map/ppermute | solution.py:213
  13.2 1.5 %copy.14 = bf16[32,8,8,256]{3,1,2,0:T(8,128)(2,1)S(1)} copy(bf16[32,8,8,256]{3,2,1,0:T(8,128)(2,1)} %bitcast.10) | data formatting | bytes 2097152
  14.7 0.0 copy-start.14
  14.7 0.0 copy-done.6
  14.8 0.0 copy-done.5
  14.8 0.0 copy-done.8
  14.8 0.0 copy-done.7
  14.8 0.0 copy-done
  14.8 3.5 %climb.1 = f32[1024,128]{1,0:T(8,128)} custom-call(bf16[512,128]{1,0:T(8,128)(2,1)S(1)} %copy-done.5, bf16[512,128]{1,0:T(8,128)(2,1)S(1)} %copy-done.6, bf16[128,256]{1,0:T(8,128)(2,1)S(1)} %copy-done.7, bf16[256,128]{1,0:T(8,128)(2,1)S(1)} %copy-done.8, bf16[8,256,256]{2,1,0:T(8,128)(2,1)S(1)} %copy-done, bf16[256,2048]{1,0:T(8,128)(2,1)S(1)} %bitcast.6), custom_call_target="tpu_custom_call" | custom-call | tf_op jit(solution)/shard_map/climb/pallas_call | solution.py:219
  18.3 6.5 %all-to-all-start = ((f32[128,8,128]{2,1,0:T(8,128)}), f32[128,8,128]{2,1,0:T(8,128)S(1)}, u32[]{:S(2)}, u32[]{:S(2)}) async-start(f32[128,8,128]{2,1,0:T(8,128)} %bitcast.1), calls=%async_computation | async-start | bytes 1048576 | tf_op jit(solution)/shard_map/all_to_all | solution.py:228
  24.8 0.0 copy-done.14
  24.8 0.1 copy.13
  24.8 0.0 collective-permute-done.recv_e
  24.8 0.0 copy-start.17
  24.8 0.6 copy-done.17
  25.5 0.0 collective-permute-done.1.recv_o
  25.5 0.0 copy-start.19
  25.5 0.6 copy-done.19
  26.1 0.0 copy-start.1
  26.1 1.6 %copy-done.1 = bf16[16,256,256]{2,1,0:T(8,128)(2,1)S(1)} copy-done((bf16[16,256,256]{2,1,0:T(8,128)(2,1)S(1)}, bf16[16,256,256]{2,1,0:T(8,128)(2,1)}, u32[]{:S(2)}) %copy-start.1) | copy-done | bytes 2097176
  27.7 0.0 copy-start.13
  27.7 0.8 copy-done.13
  28.6 0.0 copy-start.15
  28.6 0.8 copy-done.15
  29.3 1.2 %copy-done.16 = bf16[27,128,128]{2,1,0:T(8,128)(2,1)S(1)} copy-done((bf16[27,128,128]{2,1,0:T(8,128)(2,1)S(1)}, bf16[27,128,128]{2,1,0:T(8,128)(2,1)}, u32[]{:S(2)}) %copy-start.16) | copy-done | bytes 884760
  30.5 0.9 copy-done.18
  31.4 0.9 copy-done.20
  32.3 46.3 %near_far.1 = (f32[512,256]{1,0:T(8,128)S(1)}, f32[512,128]{1,0:T(8,128)S(1)}, f32[512,256]{1,0:T(8,128)S(1)}, f32[512,128]{1,0:T(8,128)S(1)}) custom-call(s32[1]{0:T(128)} %bitcast.place, s32[16,512]{1,0:T(8,128)S(1)} %copy-done.15, s32[27,512]{1,0:T(8,128)S(1)} %copy-done.13, bf16[512,128]{1,0:T(8,128)(2,1)S(1)} %copy-done.5, ...), custom_call_target="tpu_custom_call" | custom-call | flops 20000000000 | bytes 5242880 | tf_op jit(solution)/shard_map/near_far/pallas_call | solution.py:231
  78.5 0.8 copy-done.3
  79.3 0.7 copy-done.9
  80.0 0.7 copy-done.11
  80.7 0.0 all-to-all-done
  80.8 1.6 %copy-done.2 = bf16[16,256,256]{2,1,0:T(8,128)(2,1)S(1)} copy-done((bf16[16,256,256]{2,1,0:T(8,128)(2,1)S(1)}, bf16[16,256,256]{2,1,0:T(8,128)(2,1)}, u32[]{:S(2)}) %copy-start.2) | copy-done | bytes 2097176
  82.3 1.0 %copy-done.4 = f32[512,256]{1,0:T(8,128)S(1)} copy-done((f32[512,256]{1,0:T(8,128)S(1)}, f32[512,256]{1,0:T(8,128)}, u32[]{:S(2)}) %copy-start.4) | copy-done | bytes 524312
  83.4 0.9 %copy-done.10 = f32[512,128]{1,0:T(8,128)S(1)} copy-done((f32[512,128]{1,0:T(8,128)S(1)}, f32[512,128]{1,0:T(8,128)}, u32[]{:S(2)}) %copy-start.10) | copy-done | bytes 262168
  84.3 0.9 %copy-done.12 = f32[512,128]{1,0:T(8,128)S(1)} copy-done((f32[512,128]{1,0:T(8,128)S(1)}, f32[512,128]{1,0:T(8,128)}, u32[]{:S(2)}) %copy-start.12) | copy-done | bytes 262168
  85.3 5.9 %fall.1 = (f32[512,128]{1,0:T(8,128)}, f32[512,128]{1,0:T(8,128)}) custom-call(s32[1]{0:T(128)} %bitcast.place, f32[1024,128]{1,0:T(8,128)S(1)} %bitcast.8, s32[16,16]{1,0:T(8,128)S(1)} %copy-done.14, s32[16,16]{1,0:T(8,128)S(1)} %bitcast.9, bf16[8,256,256]{2,1,0:T(8,128)(2,1)S(1)} %copy-done, bf16[16,256,256]{2,1,0:T(8,128)(2,1)S(1)} %copy-done.2, ...), custom_call_target="tpu_custom_call" | custom-call | tf_op jit(solution)/shard_map/fall/pallas_call | solution.py:257
  (14 shorter events, 0.0 us)
Async XLA Ops:
  0.6 14.1 %copy-start.6 = (bf16[512,128]{1,0:T(8,128)(2,1)S(1)}, bf16[512,128]{1,0:T(8,128)(2,1)}, u32[]{:S(2)}) copy-start(bf16[512,128]{1,0:T(8,128)(2,1)} %cot.3) | copy-start | bytes 393220
  0.6 14.1 %copy-start.5 = (bf16[512,128]{1,0:T(8,128)(2,1)S(1)}, bf16[512,128]{1,0:T(8,128)(2,1)}, u32[]{:S(2)}) copy-start(bf16[512,128]{1,0:T(8,128)(2,1)} %dens.3) | copy-start | bytes 393220
  0.7 14.1 %copy-start.8 = (bf16[256,128]{1,0:T(8,128)(2,1)S(1)}, bf16[256,128]{1,0:T(8,128)(2,1)}, u32[]{:S(2)}) copy-start(bf16[256,128]{1,0:T(8,128)(2,1)} %to_v.5) | copy-start | bytes 196612
  0.7 14.1 %copy-start.7 = (bf16[128,256]{1,0:T(8,128)(2,1)S(1)}, bf16[128,256]{1,0:T(8,128)(2,1)}, u32[]{:S(2)}) copy-start(bf16[128,256]{1,0:T(8,128)(2,1)} %to_m.5) | copy-start | bytes 196612
  0.7 14.1 %copy-start = (bf16[8,256,256]{2,1,0:T(8,128)(2,1)S(1)}, bf16[8,256,256]{2,1,0:T(8,128)(2,1)}, u32[]{:S(2)}) copy-start(bf16[8,256,256]{2,1,0:T(8,128)(2,1)} %merge.3) | copy-start | bytes 3145732
  3.4 21.4 %collective-permute-start = (bf16[304,128]{1,0:T(8,128)(2,1)S(1)}, bf16[304,128]{1,0:T(8,128)(2,1)S(1)}, u32[]{:S(2)}, u32[]{:S(2)}) collective-permute-start(bf16[304,128]{1,0:T(8,128)(2,1)S(1)} %pad_maximum_fusion), channel_id=1, source_target_pairs={{0,1},{1,0},{2,3},{3,2},{4,5},{5,4},{6,7},{7,6},{8,9},{9,8},{10,11... | collective-permute-start | bytes 233480 | tf_op jit(solution)/shard_map/ppermute | solution.py:209
  6.0 19.5 %collective-permute-start.1 = (bf16[304,128]{1,0:T(8,128)(2,1)S(1)}, bf16[304,128]{1,0:T(8,128)(2,1)S(1)}, u32[]{:S(2)}, u32[]{:S(2)}) collective-permute-start(bf16[304,128]{1,0:T(8,128)(2,1)S(1)} %pad_maximum_fusion.1), channel_id=1, source_target_pairs={{1,2},{3,4},{5,6},{7,8},{9,10},{11,12},{13,14},{15,16},{17,18},{19... | collective-permute-start | bytes 233480 | tf_op jit(solution)/shard_map/ppermute | solution.py:213
  14.7 10.0 %copy-start.14 = (s32[16,16]{1,0:T(8,128)S(1)}, s32[16,16]{1,0:T(8,128)}, u32[]{:S(2)}) copy-start(s32[16,16]{1,0:T(8,128)} %coarse_list.1) | copy-start | bytes 3076
  18.3 62.5 %all-to-all-start = ((f32[128,8,128]{2,1,0:T(8,128)}), f32[128,8,128]{2,1,0:T(8,128)S(1)}, u32[]{:S(2)}, u32[]{:S(2)}) async-start(f32[128,8,128]{2,1,0:T(8,128)} %bitcast.1), calls=%async_computation | async-start | bytes 1048576 | tf_op jit(solution)/shard_map/all_to_all | solution.py:228
  24.8 0.6 copy-start.17
  25.5 0.6 copy-start.19
  26.1 1.6 %copy-start.1 = (bf16[16,256,256]{2,1,0:T(8,128)(2,1)S(1)}, bf16[16,256,256]{2,1,0:T(8,128)(2,1)}, u32[]{:S(2)}) copy-start(bf16[16,256,256]{2,1,0:T(8,128)(2,1)} %far_w.3) | copy-start | bytes 6291460
  27.7 0.8 copy-start.13
  28.6 0.8 copy-start.15
  29.3 1.2 %copy-start.16 = (bf16[27,128,128]{2,1,0:T(8,128)(2,1)S(1)}, bf16[27,128,128]{2,1,0:T(8,128)(2,1)}, u32[]{:S(2)}) copy-start(bf16[27,128,128]{2,1,0:T(8,128)(2,1)} %near_w.1) | copy-start | bytes 2654212
  30.5 0.9 copy-start.18
  31.4 0.9 copy-start.20
  78.5 0.8 copy-start.3
  79.3 0.7 copy-start.9
  80.0 0.7 copy-start.11
  80.7 1.6 %copy-start.2 = (bf16[16,256,256]{2,1,0:T(8,128)(2,1)S(1)}, bf16[16,256,256]{2,1,0:T(8,128)(2,1)}, u32[]{:S(2)}) copy-start(bf16[16,256,256]{2,1,0:T(8,128)(2,1)} %far_w.3) | copy-start | bytes 6291460
  82.3 1.0 %copy-start.4 = (f32[512,256]{1,0:T(8,128)S(1)}, f32[512,256]{1,0:T(8,128)}, u32[]{:S(2)}) copy-start(f32[512,256]{1,0:T(8,128)} %copy-done.3) | copy-start | bytes 1572868
  83.4 0.9 %copy-start.10 = (f32[512,128]{1,0:T(8,128)S(1)}, f32[512,128]{1,0:T(8,128)}, u32[]{:S(2)}) copy-start(f32[512,128]{1,0:T(8,128)} %copy-done.9) | copy-start | bytes 786436
  84.3 0.9 %copy-start.12 = (f32[512,128]{1,0:T(8,128)S(1)}, f32[512,128]{1,0:T(8,128)}, u32[]{:S(2)}) copy-start(f32[512,128]{1,0:T(8,128)} %copy-done.11) | copy-start | bytes 786436
where the time goes:
time: 91.9 us; the launch traced here: 91.2 us
  Pallas kernels  55.7 us (61%)
  local copies, waits for them, and re-layouts  16.7 us (18%)
  starting transfers between devices  16.2 us (18%)
  other arithmetic  1.81 us (2%)
    pallas_call x1, Pallas kernels, per_device(): pl.pallas_call(near_far_kernel, out_shape=[jax.ShapeDtypeStruct((rows, k)...  46.3 us
    unnamed x44, local copies, waits for them, and re-layouts  15.8 us
    ppermute x1, starting transfers between devices, per_device(): lax.ppermute(edge(odd, densities, cotangents, lists), AXES, pairs + [(b,...  7.21 us
    all_to_all x1, starting transfers between devices, per_device(): gathered = lax.all_to_all(row, AXES, 0, 0, tiled=True)  6.46 us
    pallas_call x1, Pallas kernels, per_device(): pl.pallas_call(fall_kernel, out_shape=[jax.ShapeDtypeStruct((rows, 128),...  5.89 us
    pallas_call x1, Pallas kernels, per_device(): pl.pallas_call(climb_kernel, out_shape=jax.ShapeDtypeStruct((count * 8, 1...  3.5 us
    ppermute x1, starting transfers between devices, per_device(): lax.ppermute(edge(~odd, densities, cotangents, lists), AXES, [(i, i ^ 1)...  2.55 us
  transfers between devices with their start and end apart: 3, of which 0 were waited for; matrix products, arithmetic and copies ran while one was open for 2% of the time, Pallas kernels for 55%

commit v1 on v0

v1 whole, which is shorter than its diff:
```python
import functools

import jax
import jax.numpy as jnp
from jax import lax
from jax.experimental import pallas as pl
from jax.experimental.pallas import tpu as pltpu
from jax.sharding import PartitionSpec as P

HW = 128
TILE = 256
AXES = ("coarse", "leaf")
F32 = jnp.float32
BF16 = jnp.bfloat16
NN = (((1,), (0,)), ((), ()))
NT = (((1,), (1,)), ((), ()))


def dot(a, b, dims=NN):
    return lax.dot_general(a, b, dims, preferred_element_type=F32)


def rounded(x):
    return x.astype(BF16).astype(F32)


def anywhere(count):
    return [pl.BlockSpec(memory_space=pl.ANY)] * count


def in_vmem(count):
    return [pl.BlockSpec(memory_space=pltpu.VMEM)] * count


def held(*arrays):
    return [pltpu.VMEM(a.shape, a.dtype) for a in arrays] + [pltpu.SemaphoreType.DMA((len(arrays),))]


class Fetch:
    def __init__(self, sources, targets, sems):
        self.copies = [
            pltpu.make_async_copy(s, t, sems.at[i]) for i, (s, t) in enumerate(zip(sources, targets))
        ]
        for copy in self.copies:
            copy.start()

    def wait(self, *which):
        for i in which:
            self.copies[i].wait()


def get_rows(ref, at):
    return jnp.concatenate([ref[h, at, :] for h in range(ref.shape[0])], axis=1)


def put_rows(ref, at, x):
    for h in range(ref.shape[0]):
        ref[h, at, :] = x[:, h * 128 : (h + 1) * 128]


def here():
    return lax.axis_index(AXES)


def rim(last, dens, cot, far, near, out):
    rows = dens.shape[0]
    pad = out.shape[0] - 2 * HW - far.shape[0] - near.shape[0]
    ends = []
    for at in (slice(rows - HW, rows), slice(0, HW)):
        lists = [far[:, at].astype(F32), near[:, at].astype(F32), jnp.full((pad, HW), -1.0, F32)]
        ends.append(jnp.concatenate(lists, axis=0).astype(BF16))
    out[:HW, :] = jnp.where(last, dens[rows - HW :, :], dens[:HW, :])
    out[HW : 2 * HW, :] = jnp.where(last, cot[rows - HW :, :], cot[:HW, :])
    out[2 * HW :, :] = jnp.where(last, ends[0], ends[1])


def climb_kernel(*refs):
    sources, (out, far_rim, near_rim, split_by_child), rest = refs[:8], refs[8:12], refs[12:]
    dens, cot, far, near, to_m, to_v, merge, split, sems, mom, adj, wide = rest
    fetch = Fetch(sources, rest[:8], sems)
    rows = dens.shape[0]
    k = to_m.shape[1]
    odd = lax.rem(here(), 2) == 1
    fetch.wait(0, 1, 2, 3)
    rim(odd, dens, cot, far, near, far_rim)
    rim(jnp.logical_not(odd), dens, cot, far, near, near_rim)
    fetch.wait(4, 5)
    put_rows(mom, pl.ds(0, rows), rounded(dot(dens[...], to_m[...])))
    put_rows(adj, pl.ds(0, rows), rounded(dot(cot[...], to_v[...], NT)))
    fetch.wait(6, 7)
    for h in range(2):
        wide[h] = split[:, :, h * 128 : (h + 1) * 128].astype(F32).reshape(8 * k, 128)
    for c in range(8):
        split_by_child[c] = get_rows(wide, pl.ds(c, k, stride=8)).astype(BF16)
    while rows > 1:
        rows //= 8
        up = jnp.zeros((rows, k), F32)
        adj_up = jnp.zeros((rows, k), F32)
        for c in range(8):
            child = pl.ds(c, rows, stride=8) if rows > 1 else pl.ds(c, 1)
            up += dot(get_rows(mom, child).astype(BF16), merge[c])
            adj_up += dot(get_rows(adj, child).astype(BF16), split_by_child[c], NT)
        put_rows(mom, pl.ds(0, rows), rounded(up))
        put_rows(adj, pl.ds(0, rows), rounded(adj_up))
    row = jnp.concatenate([mom[0, :1], mom[1, :1], adj[0, :1], adj[1, :1], jnp.zeros((4, 128), F32)], axis=0)
    out[...] = jnp.broadcast_to(row[None], (out.shape[0] // 8, 8, 128)).reshape(out.shape)


def near_far_kernel(*refs):
    sources, (potential, gradient), rest = refs[:10], refs[10:12], refs[12:]
    recv_e, recv_o, far, near, dens, cot, to_m, to_v, far_w, near_w, sems = rest[:11]
    dens_wide, cot_wide, mom_wide, adj_wide, row_targets, col_targets = rest[11:17]
    dens_pair, far_picked, far_collected, near_picked, near_collected, far_wt, near_wt = rest[17:]
    fetch = Fetch(sources, rest[:10], sems)
    fetch.wait(0, 1, 2, 3, 4, 5, 6, 7)
    rows = dens.shape[0]
    wide = rows + 2 * HW
    n_far, n_near = far.shape[0], near.shape[0]
    slots = n_far + n_near
    odd = lax.rem(here(), 2) == 1
    first, second = recv_e[...], recv_o[...]
    left = jnp.where(odd, first, second)
    right = jnp.where(odd, second, first)
    for target, own, start in ((dens_wide, dens, 0), (cot_wide, cot, HW)):
        target[:HW, :] = left[start : start + HW]
        target[HW : HW + rows, :] = own[...]
        target[HW + rows :, :] = right[start : start + HW]
    mom_wide[...] = dot(dens_wide[...], to_m[...]).astype(BF16)
    adj_wide[...] = dot(cot_wide[...], to_v[...], NT).astype(BF16)

    padded = row_targets.shape[0]
    row_targets[...] = jnp.full(row_targets.shape, -1.0, F32)
    row_targets[:, :HW] = left[2 * HW :].astype(F32)
    row_targets[:n_far, HW : HW + rows] = far[...].astype(F32)
    row_targets[n_far:slots, HW : HW + rows] = near[...].astype(F32)
    row_targets[:, HW + rows :] = right[2 * HW :].astype(F32)
    own = row_targets[:, HW : HW + rows]
    own = jnp.concatenate([own, jnp.full((128 - padded, rows), -1.0, F32)], axis=0)
    own = own.T
    place_r = (lax.broadcasted_iota(jnp.int32, own.shape, 0) % TILE).astype(F32)
    col_targets[...] = jnp.where(own >= 0, own + place_r, -1.0)
    entries = row_targets[...]
    place_w = (lax.broadcasted_iota(jnp.int32, entries.shape, 1) % TILE).astype(F32)
    row_targets[...] = jnp.where(entries >= 0, entries + place_w, -1.0)

    lane = lax.broadcasted_iota(jnp.int32, (TILE, 128), 1).astype(F32)
    lanes = [lane.astype(BF16), (lane + 128.0).astype(BF16)]
    down = lax.broadcasted_iota(jnp.int32, (TILE, TILE), 0).astype(F32).astype(BF16)
    one = jnp.ones((), BF16)
    zero = jnp.zeros((), BF16)
    blocks = rows // TILE
    for p in range(blocks):
        dens_pair[p, :, :128] = dens_wide[p * TILE : (p + 1) * TILE, :]
        dens_pair[p, :, 128:] = dens_wide[(p + 1) * TILE : (p + 2) * TILE, :]

    def column_of(slot, p):
        column = col_targets[p * TILE : (p + 1) * TILE, :]
        return jnp.take_along_axis(column, jnp.full(column.shape, slot, jnp.int32), axis=1)

    def table_of(slot, p):
        column = column_of(slot, p)
        low, high = column.astype(BF16), (column - TILE).astype(BF16)
        return jnp.concatenate(
            [jnp.where(c == t, one, zero) for t in (low, high) for c in lanes], axis=1
        )

    def scatter_table_of(slot, p):
        entry = row_targets[pl.ds(slot, 1), p * TILE : (p + 2) * TILE]
        high = jnp.broadcast_to(entry[:, :TILE] - TILE, (TILE, TILE)).astype(BF16)
        low = jnp.broadcast_to(entry[:, TILE:], (TILE, TILE)).astype(BF16)
        return jnp.concatenate([jnp.where(down == t, one, zero) for t in (high, low)], axis=1)

    fetch.wait(8, 9)

    @pl.loop(0, n_far, unroll=4)
    def _(j):
        at = pl.ds(pl.multiple_of(j * TILE, TILE), TILE)
        for p in range(blocks):
            own, reach = pl.ds(p * TILE, TILE), pl.ds(p * TILE, 2 * TILE)
            far_picked[own, at] = dot(table_of(j, p), mom_wide[reach, :]).astype(BF16)
            far_collected[own, at] = dot(scatter_table_of(j, p), adj_wide[reach, :]).astype(BF16)
        far_wt[pl.ds(pl.multiple_of(j * TILE, TILE), TILE), :] = far_w[j].T

    @pl.loop(0, n_near, unroll=9)
    def _(j):
        at = pl.ds(pl.multiple_of(j * 128, 128), 128)
        for p in range(blocks):
            own, reach = pl.ds(p * TILE, TILE), pl.ds(p * TILE, 2 * TILE)
            column = column_of(j + n_far, p)
            second = column >= TILE
            place = jnp.where(second, column - TILE, column).astype(BF16)
            table = jnp.concatenate([jnp.where(c == place, one, zero) for c in lanes], axis=1)
            both = dot(table, dens_pair[p])
            near_picked[own, at] = jnp.where(second, both[:, 128:], both[:, :128]).astype(BF16)
            near_collected[own, at] = dot(scatter_table_of(j + n_far, p), cot_wide[reach, :]).astype(BF16)
        near_wt[pl.ds(pl.multiple_of(j * 128, 128), 128), :] = near_w[j].T

    leaf_far = dot(far_picked[...], far_w[...].reshape(far_wt.shape)).astype(BF16)
    adj_far = dot(far_collected[...], far_wt[...]).astype(BF16)
    near_val = dot(near_picked[...], near_w[...].reshape(near_wt.shape))
    near_adj = dot(near_collected[...], near_wt[...])
    potential[...] = dot(leaf_far, to_v[...]) + near_val
    gradient[...] = dot(adj_far, to_m[...], NT) + near_adj


def fall_kernel(*refs):
    sources, (potential, gradient), rest = refs[:9], refs[9:11], refs[11:]
    gathered, coarse_list, merge, split, far_w, to_m, to_v, near_pot, near_grad, sems, fall, adj_fall = rest
    fetch = Fetch(sources, rest[:9], sems)
    fetch.wait(0, 1, 2, 3)
    k = merge.shape[2]
    boxes = coarse_list.shape[1]
    coarse_m = jnp.zeros((boxes, k), F32)
    coarse_a = jnp.zeros((boxes, k), F32)
    for c in range(8):
        parts = [gathered[pl.ds(8 * c + i, boxes, stride=64), :] for i in range(4)]
        moments = jnp.concatenate(parts[:2], axis=1).astype(BF16)
        adjoints = jnp.concatenate(parts[2:], axis=1).astype(BF16)
        coarse_m += dot(moments, merge[c])
        coarse_a += dot(adjoints, split[c], NT)
    coarse_m = coarse_m.astype(BF16)
    coarse_a = coarse_a.astype(BF16)
    local = jnp.zeros((boxes, k), F32)
    adjoint = jnp.zeros((boxes, k), F32)
    fetch.wait(4)
    coarse_list_t = jnp.concatenate(
        [coarse_list[...].astype(F32), jnp.full((boxes, 128 - boxes), -1.0, F32)], axis=1
    )
    coarse_list_t = jnp.concatenate([coarse_list_t, jnp.full((128 - boxes, 128), -1.0, F32)], axis=0).T
    coarse_list_t = coarse_list_t[:boxes, :].astype(jnp.int32)
    across = lax.broadcasted_iota(jnp.int32, (boxes, boxes), 1)
    along = lax.broadcasted_iota(jnp.int32, (boxes, boxes), 0)
    for j in range(far_w.shape[0]):
        table = jnp.where(across == coarse_list_t[:, j : j + 1], 1.0, 0.0).astype(BF16)
        local += dot(dot(table, coarse_m).astype(BF16), far_w[j])
        table = jnp.where(along == coarse_list[j : j + 1, :], 1.0, 0.0).astype(BF16)
        adjoint += dot(dot(table, coarse_a).astype(BF16), far_w[j], NT)
    put_rows(fall, pl.ds(0, boxes), rounded(local))
    put_rows(adj_fall, pl.ds(0, boxes), rounded(adjoint))
    box, child = here() // 8, lax.rem(here(), 8)
    top = get_rows(fall, pl.ds(box, 1)).astype(BF16)
    adj_top = get_rows(adj_fall, pl.ds(box, 1)).astype(BF16)
    put_rows(fall, pl.ds(0, 1), rounded(dot(top, split[child])))
    put_rows(adj_fall, pl.ds(0, 1), rounded(dot(adj_top, merge[child], NT)))
    rows = 1
    while rows < fall.shape[1]:
        parents = get_rows(fall, pl.ds(0, rows)).astype(BF16)
        adj_parents = get_rows(adj_fall, pl.ds(0, rows)).astype(BF16)
        for c in range(8):
            children = pl.ds(c, rows, stride=8) if rows > 1 else pl.ds(c, 1)
            put_rows(fall, children, rounded(dot(parents, split[c])))
            put_rows(adj_fall, children, rounded(dot(adj_parents, merge[c], NT)))
        rows *= 8
    fetch.wait(5, 6, 7, 8)
    potential[...] = dot(get_rows(fall, pl.ds(0, rows)).astype(BF16), to_v[...]) + near_pot[...]
    gradient[...] = dot(get_rows(adj_fall, pl.ds(0, rows)).astype(BF16), to_m[...], NT) + near_grad[...]


def near_far_call(far, near, dens, cot, recv_e, recv_o, to_m, to_v, far_w, near_w):
    rows = dens.shape[0]
    k = to_m.shape[1]
    padded = recv_e.shape[0] - 2 * HW
    wide = rows + 2 * HW
    operands = (recv_e, recv_o, far, near, dens, cot, to_m, to_v, far_w, near_w)
    return pl.pallas_call(
        near_far_kernel,
        out_shape=[jax.ShapeDtypeStruct((rows, 128), F32)] * 2,
        in_specs=anywhere(10),
        out_specs=in_vmem(2),
        scratch_shapes=held(*operands)
        + [
            pltpu.VMEM((wide, 128), BF16),
            pltpu.VMEM((wide, 128), BF16),
            pltpu.VMEM((wide, k), BF16),
            pltpu.VMEM((wide, k), BF16),
            pltpu.VMEM((padded, wide), F32),
            pltpu.VMEM((rows, 128), F32),
            pltpu.VMEM((rows // TILE, TILE, 256), BF16),
            pltpu.VMEM((rows, far.shape[0] * k), BF16),
            pltpu.VMEM((rows, far.shape[0] * k), BF16),
            pltpu.VMEM((rows, near.shape[0] * 128), BF16),
            pltpu.VMEM((rows, near.shape[0] * 128), BF16),
            pltpu.VMEM((far.shape[0] * k, k), BF16),
            pltpu.VMEM((near.shape[0] * 128, 128), BF16),
        ],
        compiler_params=pltpu.CompilerParams(vmem_limit_bytes=64 << 20),
        cost_estimate=pl.CostEstimate(flops=20 * 10**9, bytes_accessed=5 << 20, transcendentals=0),
        name="near_far",
    )(*operands)


def per_device(
    densities, cotangents, far_list, near_list, coarse_list,
    to_moments, merge_moments, far_translate, local_split, to_values, near_blocks,
):
    rows = densities.shape[0]
    k = to_moments.shape[1]
    count = lax.axis_size(AXES)
    slots = far_list.shape[0] + near_list.shape[0]
    rim_shape = jax.ShapeDtypeStruct((2 * HW + -(-slots // 16) * 16, 128), BF16)
    chain = pltpu.VMEM((k // 128, rows, 128), F32)
    operands = (
        densities, cotangents, far_list, near_list, to_moments, to_values, merge_moments, local_split,
    )
    row, far_rim, near_rim, split = pl.pallas_call(
        climb_kernel,
        out_shape=[
            jax.ShapeDtypeStruct((count * 8, 128), F32),
            rim_shape,
            rim_shape,
            jax.ShapeDtypeStruct((8, k, k), BF16),
        ],
        in_specs=anywhere(8),
        out_specs=in_vmem(4),
        scratch_shapes=held(*operands) + [chain, chain, pltpu.VMEM((k // 128, 8 * k, 128), F32)],
        compiler_params=pltpu.CompilerParams(vmem_limit_bytes=64 << 20),
        name="climb",
    )(*operands)
    pairs = [(i, i + 1) for i in range(1, count - 1, 2)]
    recv_o = lax.ppermute(far_rim, AXES, pairs + [(b, a) for a, b in pairs])
    recv_e = lax.ppermute(near_rim, AXES, [(i, i ^ 1) for i in range(count)])
    gathered = lax.all_to_all(row, AXES, 0, 0, tiled=True)
    sums = near_far_call(
        far_list, near_list, densities, cotangents, recv_e, recv_o,
        to_moments, to_values, far_translate, near_blocks,
    )
    operands = (
        gathered, coarse_list, merge_moments, split, far_translate, to_moments, to_values, *sums,
    )
    return pl.pallas_call(
        fall_kernel,
        out_shape=[jax.ShapeDtypeStruct((rows, 128), F32)] * 2,
        in_specs=anywhere(9),
        out_specs=in_vmem(2),
        scratch_shapes=held(*operands) + [chain, chain],
        compiler_params=pltpu.CompilerParams(vmem_limit_bytes=64 << 20),
        name="fall",
    )(*operands)


def solution(mesh):
    rows = P(AXES, None)
    lists = P(None, AXES)
    return jax.shard_map(
        per_device,
        mesh=mesh,
        in_specs=(rows, rows, lists, lists) + (P(),) * 7,
        out_specs=(rows, rows),
        check_vma=False,
    )
```

time: 91.9 us -> 49.6 us (0.54)
  Pallas kernels: 55.7 us -> 31.9 us
  local copies, waits for them, and re-layouts: 16.7 us -> 0 us
  other arithmetic: 1.81 us -> 0 us
    pallas_call x2, Pallas kernels: 49.8 us -> 23.9 us  [the longest x1 18.6 us: near_far_call(): pl.pallas_call(near_far_kernel, out_shape=[jax.ShapeDtypeStruct((rows, 12...]
    unnamed x44 -> x0, local copies, waits for them, and re-layouts: 15.8 us -> none
    pallas_call x1, Pallas kernels: 5.89 us -> 7.98 us  [per_device(): pl.pallas_call(fall_kernel, out_shape=[jax.ShapeDtypeStruct((rows, 128),...]
    another operation x2 -> x0, other arithmetic: 1.72 us -> none
  transfers between devices with their start and end apart: 3 -> 3, of which waited for: 0 -> 0; matrix products, arithmetic and copies ran while one was open for 2% -> 0% of each run, Pallas kernels for 55% -> 38%
where the time goes in v1:
time: 49.6 us; the launch traced here: 49.4 us
  Pallas kernels  31.9 us (64%)
  starting transfers between devices  16.7 us (34%)
  between operations  0.85 us (2%)
    pallas_call x1, Pallas kernels, near_far_call(): pl.pallas_call(near_far_kernel, out_shape=[jax.ShapeDtypeStruct((rows, 12...  18.6 us
    pallas_call x1, Pallas kernels, per_device(): pl.pallas_call(fall_kernel, out_shape=[jax.ShapeDtypeStruct((rows, 128),...  7.98 us
    ppermute x1, starting transfers between devices, per_device(): recv_o = lax.ppermute(far_rim, AXES, pairs + [(b, a) for a, b in pairs])  7.21 us
    all_to_all x1, starting transfers between devices, per_device(): gathered = lax.all_to_all(row, AXES, 0, 0, tiled=True)  6.94 us
    pallas_call x1, Pallas kernels, per_device(): pl.pallas_call(climb_kernel, out_shape=[jax.ShapeDtypeStruct((count * 8,...  5.33 us
    ppermute x1, starting transfers between devices, per_device(): recv_e = lax.ppermute(near_rim, AXES, [(i, i ^ 1) for i in range(count)])  2.55 us
  transfers between devices with their start and end apart: 3, of which 0 were waited for; matrix products, arithmetic and copies ran while one was open for 0% of the time, Pallas kernels for 38%

profile of v1, /device:TPU:1, one launch (start us, length us, event | category | flops | bytes accessed | tf_op | source)
XLA Modules:
  0.0 49.4 jit_solution(4749495874956418373)
XLA Ops:
  0.6 5.3 %climb.1 = (f32[1024,128]{1,0:T(8,128)}, bf16[304,128]{1,0:T(8,128)(2,1)}, bf16[304,128]{1,0:T(8,128)(2,1)}, bf16[8,256,256]{2,1,0:T(8,128)(2,1)}) custom-call(bf16[512,128]{1,0:T(8,128)(2,1)} %refs_4_.4, bf16[512,128]{1,0:T(8,128)(2,1)} %refs_5_.4, s32[16,512]{1,0:T(8,128)} %refs_2_.4, s32[27,512]{1,0:T(8,128)} %refs_3_.3, bf16[128,256]{1,0:T(8,128)(2,1)} %refs_5_.5, ...), custom_call_target="tpu_custom_call" | custom-call | tf_op jit(solution)/shard_map/climb/pallas_call | solution.py:305
  6.0 2.5 %collective-permute-start = (bf16[304,128]{1,0:T(8,128)(2,1)}, bf16[304,128]{1,0:T(8,128)(2,1)}, u32[]{:S(2)}, u32[]{:S(2)}) collective-permute-start(bf16[304,128]{1,0:T(8,128)(2,1)} %get-tuple-element.10), channel_id=1, source_target_pairs={{0,1},{1,0},{2,3},{3,2},{4,5},{5,4},{6,7},{7,6},{8,9},{9,8},{10,11... | collective-permute-start | bytes 233480 | tf_op jit(solution)/shard_map/ppermute | solution.py:321
  8.5 7.2 %collective-permute-start.1 = (bf16[304,128]{1,0:T(8,128)(2,1)}, bf16[304,128]{1,0:T(8,128)(2,1)}, u32[]{:S(2)}, u32[]{:S(2)}) collective-permute-start(bf16[304,128]{1,0:T(8,128)(2,1)} %get-tuple-element.11), channel_id=1, source_target_pairs={{1,2},{3,4},{5,6},{7,8},{9,10},{11,12},{13,14},{15,16},{17,18},{19... | collective-permute-start | bytes 233480 | tf_op jit(solution)/shard_map/ppermute | solution.py:320
  15.7 6.9 %all-to-all-start = ((f32[128,8,128]{2,1,0:T(8,128)}), f32[128,8,128]{2,1,0:T(8,128)}, u32[]{:S(2)}, u32[]{:S(2)}) async-start(f32[128,8,128]{2,1,0:T(8,128)} %bitcast.2), calls=%async_computation | async-start | bytes 1048576 | tf_op jit(solution)/shard_map/all_to_all | solution.py:322
  22.7 0.0 collective-permute-done.refs_0_
  22.7 0.0 collective-permute-done.1.refs_1_
  22.7 18.6 %near_far.1 = (f32[512,128]{1,0:T(8,128)}, f32[512,128]{1,0:T(8,128)}) custom-call(bf16[304,128]{1,0:T(8,128)(2,1)} %collective-permute-done.refs_0_, bf16[304,128]{1,0:T(8,128)(2,1)} %collective-permute-done.1.refs_1_, s32[16,512]{1,0:T(8,128)} %refs_2_.4, s32[27,512]{1,0:T(8,128)} %refs_3_.3, bf16[512,128]{1,0:T(8,128)(2,1)} %refs_4_.4, ...), custom_call_target="tpu_custom_call" | custom-call | flops 20000000000 | bytes 5242880 | tf_op jit(solution)/shard_map/near_far/pallas_call | solution.py:265
  41.3 0.0 all-to-all-done
  41.3 8.0 %fall.1 = (f32[512,128]{1,0:T(8,128)}, f32[512,128]{1,0:T(8,128)}) custom-call(f32[1024,128]{1,0:T(8,128)} %bitcast.1.refs_0_, s32[16,16]{1,0:T(8,128)} %refs_1_.3, bf16[8,256,256]{2,1,0:T(8,128)(2,1)} %refs_2_.5, bf16[8,256,256]{2,1,0:T(8,128)(2,1)} %get-tuple-element.9.refs_3_, bf16[16,256,256]{2,1,0:T(8,128)(2,1)} %refs_4_.5, bf16[128,256]{1,0:T(8,128)(2,1)} %refs_5_.5, ...), custom_call_target="tpu_custom_call" | custom-call | tf_op jit(solution)/shard_map/fall/pallas_call | solution.py:330
Async XLA Ops:
  6.0 16.7 %collective-permute-start = (bf16[304,128]{1,0:T(8,128)(2,1)}, bf16[304,128]{1,0:T(8,128)(2,1)}, u32[]{:S(2)}, u32[]{:S(2)}) collective-permute-start(bf16[304,128]{1,0:T(8,128)(2,1)} %get-tuple-element.10), channel_id=1, source_target_pairs={{0,1},{1,0},{2,3},{3,2},{4,5},{5,4},{6,7},{7,6},{8,9},{9,8},{10,11... | collective-permute-start | bytes 233480 | tf_op jit(solution)/shard_map/ppermute | solution.py:321
  8.5 14.2 %collective-permute-start.1 = (bf16[304,128]{1,0:T(8,128)(2,1)}, bf16[304,128]{1,0:T(8,128)(2,1)}, u32[]{:S(2)}, u32[]{:S(2)}) collective-permute-start(bf16[304,128]{1,0:T(8,128)(2,1)} %get-tuple-element.11), channel_id=1, source_target_pairs={{1,2},{3,4},{5,6},{7,8},{9,10},{11,12},{13,14},{15,16},{17,18},{19... | collective-permute-start | bytes 233480 | tf_op jit(solution)/shard_map/ppermute | solution.py:320
  15.7 25.5 %all-to-all-start = ((f32[128,8,128]{2,1,0:T(8,128)}), f32[128,8,128]{2,1,0:T(8,128)}, u32[]{:S(2)}, u32[]{:S(2)}) async-start(f32[128,8,128]{2,1,0:T(8,128)} %bitcast.2), calls=%async_computation | async-start | bytes 1048576 | tf_op jit(solution)/shard_map/all_to_all | solution.py:322

commit v2 on v1

v2 whole, which is shorter than its diff:
```python
import functools

import jax
import jax.numpy as jnp
from jax import lax
from jax.experimental import pallas as pl
from jax.experimental.pallas import tpu as pltpu
from jax.sharding import PartitionSpec as P

HW = 128
TILE = 256
PAIR = 8
AXES = ("coarse", "leaf")
F32 = jnp.float32
BF16 = jnp.bfloat16
NN = (((1,), (0,)), ((), ()))
NT = (((1,), (1,)), ((), ()))


def dot(a, b, dims=NN):
    return lax.dot_general(a, b, dims, preferred_element_type=F32)


def rounded(x):
    return x.astype(BF16).astype(F32)


def anywhere(count):
    return [pl.BlockSpec(memory_space=pl.ANY)] * count


def in_vmem(count):
    return [pl.BlockSpec(memory_space=pltpu.VMEM)] * count


def held(*arrays):
    return [pltpu.VMEM(a.shape, a.dtype) for a in arrays] + [pltpu.SemaphoreType.DMA((len(arrays),))]


class Fetch:
    def __init__(self, sources, targets, sems):
        self.copies = [
            pltpu.make_async_copy(s, t, sems.at[i]) for i, (s, t) in enumerate(zip(sources, targets))
        ]
        for copy in self.copies:
            copy.start()

    def wait(self, *which):
        for i in which:
            self.copies[i].wait()


def get_rows(ref, at):
    return jnp.concatenate([ref[h, at, :] for h in range(ref.shape[0])], axis=1)


def put_rows(ref, at, x):
    for h in range(ref.shape[0]):
        ref[h, at, :] = x[:, h * 128 : (h + 1) * 128]


def here():
    return lax.axis_index(AXES)


def rim(last, dens, cot, far, near, out):
    rows = dens.shape[0]
    pad = out.shape[0] - 2 * HW - far.shape[0] - near.shape[0]
    ends = []
    for at in (slice(rows - HW, rows), slice(0, HW)):
        lists = [far[:, at].astype(F32), near[:, at].astype(F32), jnp.full((pad, HW), -1.0, F32)]
        ends.append(jnp.concatenate(lists, axis=0).astype(BF16))
    out[:HW, :] = jnp.where(last, dens[rows - HW :, :], dens[:HW, :])
    out[HW : 2 * HW, :] = jnp.where(last, cot[rows - HW :, :], cot[:HW, :])
    out[2 * HW :, :] = jnp.where(last, ends[0], ends[1])


def climb_kernel(*refs):
    sources, (out, far_rim, near_rim, split_by_child), rest = refs[:8], refs[8:12], refs[12:]
    dens, cot, far, near, to_m, to_v, merge, split, sems, mom, adj, wide = rest
    fetch = Fetch(sources, rest[:8], sems)
    rows = dens.shape[0]
    k = to_m.shape[1]
    odd = lax.rem(here(), 2) == 1
    fetch.wait(0, 1, 2, 3)
    rim(odd, dens, cot, far, near, far_rim)
    rim(jnp.logical_not(odd), dens, cot, far, near, near_rim)
    fetch.wait(4, 5)
    put_rows(mom, pl.ds(0, rows), rounded(dot(dens[...], to_m[...])))
    put_rows(adj, pl.ds(0, rows), rounded(dot(cot[...], to_v[...], NT)))
    fetch.wait(6, 7)
    for h in range(2):
        wide[h] = split[:, :, h * 128 : (h + 1) * 128].astype(F32).reshape(8 * k, 128)
    for c in range(8):
        split_by_child[c] = get_rows(wide, pl.ds(c, k, stride=8)).astype(BF16)
    while rows > 1:
        rows //= 8
        adj_up = jnp.zeros((rows, k), F32)
        children = [pl.ds(c, rows, stride=8) if rows > 1 else pl.ds(c, 1) for c in range(8)]
        up = jnp.concatenate([get_rows(mom, child) for child in children], axis=1).astype(BF16)
        up = dot(up, merge[...].reshape(8 * k, k))
        for c, child in enumerate(children):
            adj_up += dot(get_rows(adj, child).astype(BF16), split_by_child[c], NT)
        put_rows(mom, pl.ds(0, rows), rounded(up))
        put_rows(adj, pl.ds(0, rows), rounded(adj_up))
    row = jnp.concatenate([mom[0, :1], mom[1, :1], adj[0, :1], adj[1, :1], jnp.zeros((4, 128), F32)], axis=0)
    out[...] = jnp.broadcast_to(row[None], (out.shape[0] // 8, 8, 128)).reshape(out.shape)


def near_far_kernel(*refs):
    sources, (potential, gradient), rest = refs[:10], refs[10:12], refs[12:]
    recv_e, recv_o, far, near, dens, cot, near_w, to_m, to_v, far_w, sems = rest[:11]
    dens_pair, cot_rim, row_place, rim_place, col_targets, picked, collected = rest[11:18]
    near_wt, far_half, far_op, far_opt = rest[18:]
    fetch = Fetch(sources, rest[:10], sems)
    rows = dens.shape[0]
    blocks = rows // TILE
    n_far, n_near = far.shape[0], near.shape[0]
    slots = n_far + n_near
    padded = row_place.shape[0]
    fetch.wait(0, 1, 2, 3, 4, 5)
    odd = lax.rem(here(), 2) == 1
    first, second = recv_e[...], recv_o[...]
    left = jnp.where(odd, first, second)
    right = jnp.where(odd, second, first)
    dens_wide = [left[:HW]] + [dens[i * HW : (i + 1) * HW, :] for i in range(rows // HW)] + [right[:HW]]
    for p in range(blocks):
        for i in range(4):
            at = slice((i % 2) * HW, (i % 2 + 1) * HW)
            dens_pair[p, at, (i // 2) * 128 : (i // 2 + 1) * 128] = dens_wide[2 * p + i]
    cot_rim[...] = jnp.zeros(cot_rim.shape, BF16)
    cot_rim[:HW, :128] = left[HW : 2 * HW]
    cot_rim[HW:, 128:] = right[HW : 2 * HW]

    listed = jnp.concatenate(
        [far[...].astype(F32), near[...].astype(F32), jnp.full((128 - slots, rows), -1.0, F32)], axis=0
    )
    place = (lax.broadcasted_iota(jnp.int32, listed.shape, 1) % TILE).astype(F32)
    listed = jnp.where(listed >= 0, listed + place, -1.0)
    col_targets[...] = listed.T
    listed = listed[:padded]
    row_place[...] = jnp.where(listed >= TILE, listed - TILE, listed)
    listed = jnp.concatenate([left[2 * HW :].astype(F32), right[2 * HW :].astype(F32)], axis=1)
    lane = lax.broadcasted_iota(jnp.int32, listed.shape, 1)
    place = jnp.where(lane < HW, lane - TILE, lane - HW).astype(F32)
    rim_place[...] = jnp.where(listed >= 0, listed + place, -1.0)

    lane = lax.broadcasted_iota(jnp.int32, (TILE, 128), 1).astype(F32)
    lanes = [lane.astype(BF16), (lane + 128.0).astype(BF16)]
    down = lax.broadcasted_iota(jnp.int32, (TILE, TILE), 0).astype(F32).astype(BF16)
    one = jnp.ones((), BF16)
    zero = jnp.zeros((), BF16)

    def step(slot):
        at = pl.ds(pl.multiple_of(slot * 128, 128), 128)
        parts = []
        for p in range(blocks):
            own = slice(p * TILE, (p + 1) * TILE)
            column = col_targets[own, :]
            column = jnp.take_along_axis(column, jnp.full(column.shape, slot, jnp.int32), axis=1)
            upper = column >= TILE
            place = jnp.where(upper, column - TILE, column).astype(BF16)
            table = jnp.concatenate([jnp.where(c == place, one, zero) for c in lanes], axis=1)
            both = dot(table, dens_pair[p])
            picked[own, at] = jnp.where(upper, both[:, 128:], both[:, :128]).astype(BF16)
            upper = column.astype(BF16) >= jnp.full((), TILE, BF16)
            values = cot[own, :]
            halves = [jnp.where(upper, zero, values), jnp.where(upper, values, zero)]
            entry = jnp.broadcast_to(row_place[pl.ds(slot, 1), own], (TILE, TILE)).astype(BF16)
            parts.append(dot(jnp.where(down == entry, one, zero), jnp.concatenate(halves, axis=1)))
        entry = jnp.broadcast_to(rim_place[pl.ds(slot, 1), :], (HW, TILE)).astype(BF16)
        rim = dot(jnp.where(down[:HW] == entry, one, zero), cot_rim[...])
        collected[:HW, at] = (parts[0][HW:, :128] + rim[:, :128]).astype(BF16)
        for p in range(blocks - 1):
            own = slice(HW + p * TILE, HW + (p + 1) * TILE)
            collected[own, at] = (parts[p][:, 128:] + parts[p + 1][:, :128]).astype(BF16)
        collected[rows - HW :, at] = (parts[-1][:HW, 128:] + rim[:, 128:]).astype(BF16)

    @pl.loop(0, n_far, unroll=16)
    def _(j):
        step(j)

    fetch.wait(6)

    @pl.loop(0, n_near, unroll=27)
    def _(j):
        step(j + n_far)
        near_wt[pl.ds(pl.multiple_of(j * 128, 128), 128), :] = near_w[j].T

    fetch.wait(7, 8, 9)
    for j in range(n_far):
        far_half[j * 128 : (j + 1) * 128, :] = dot(to_m[...], far_w[j]).astype(BF16)
    operator = dot(far_half[...], to_v[...])
    far_op[...] = operator.astype(BF16)
    for j in range(n_far):
        far_opt[j * 128 : (j + 1) * 128, :] = operator[j * 128 : (j + 1) * 128].T.astype(BF16)
    split = n_far * 128
    near_op = near_w[...].reshape(near_wt.shape)
    potential[...] = dot(picked[:, :split], far_op[...]) + dot(picked[:, split:], near_op)
    gradient[...] = dot(collected[:, :split], far_opt[...]) + dot(collected[:, split:], near_wt[...])


def fall_kernel(*refs):
    sources, (potential, gradient), rest = refs[:9], refs[9:11], refs[11:]
    gathered, coarse_list, merge, split, far_w, to_m, to_v, near_pot, near_grad, sems, fall, adj_fall = rest
    fetch = Fetch(sources, rest[:9], sems)
    k = merge.shape[2]
    slots, boxes = coarse_list.shape
    box, child = here() // 8, lax.rem(here(), 8)
    fetch.wait(0, 1, 2)

    def children(c, first):
        at = [gathered[pl.ds(PAIR * c + first + i, boxes, stride=PAIR * 8), :] for i in range(2)]
        return jnp.concatenate(at, axis=1).astype(BF16)

    moments = jnp.concatenate([children(c, 0) for c in range(8)], axis=1)
    coarse_m = dot(moments, merge[...].reshape(8 * k, k)).astype(BF16)
    fetch.wait(3)
    coarse_a = jnp.zeros((boxes, k), F32)
    for c in range(8):
        coarse_a += dot(children(c, 2), split[c], NT)
    coarse_a = coarse_a.astype(BF16)
    listed = coarse_list[...]
    across = lax.broadcasted_iota(jnp.int32, listed.shape, 1)
    named = jnp.sum(jnp.where(across == box, listed, 0), axis=1, keepdims=True)
    picked = dot(jnp.where(across == named, 1.0, 0.0).astype(BF16), coarse_m)
    collected = dot(jnp.where(listed == box, 1.0, 0.0).astype(BF16), coarse_a).astype(BF16)
    picked = jnp.concatenate([picked[j : j + 1, :] for j in range(slots)], axis=1).astype(BF16)
    fetch.wait(4)
    operators = far_w[...].reshape(slots * k, k)
    top = dot(picked, operators).astype(BF16)
    spread = dot(collected, operators, NT)
    adj_top = spread[:1, :k]
    for j in range(1, slots):
        adj_top += spread[j : j + 1, j * k : (j + 1) * k]
    adj_top = adj_top.astype(BF16)
    put_rows(fall, pl.ds(0, 1), rounded(dot(top, split[child])))
    put_rows(adj_fall, pl.ds(0, 1), rounded(dot(adj_top, merge[child], NT)))
    rows = 1
    while rows < fall.shape[1]:
        parents = get_rows(fall, pl.ds(0, rows)).astype(BF16)
        adj_parents = get_rows(adj_fall, pl.ds(0, rows)).astype(BF16)
        adj_spread = rounded(dot(adj_parents, merge[...].reshape(8 * k, k), NT))
        for c in range(8):
            below = pl.ds(c, rows, stride=8) if rows > 1 else pl.ds(c, 1)
            put_rows(fall, below, rounded(dot(parents, split[c])))
            put_rows(adj_fall, below, adj_spread[:, c * k : (c + 1) * k])
        rows *= 8
    fetch.wait(5, 6, 7, 8)
    potential[...] = dot(get_rows(fall, pl.ds(0, rows)).astype(BF16), to_v[...]) + near_pot[...]
    gradient[...] = dot(get_rows(adj_fall, pl.ds(0, rows)).astype(BF16), to_m[...], NT) + near_grad[...]


def near_far_call(far, near, dens, cot, recv_e, recv_o, to_m, to_v, far_w, near_w):
    rows = dens.shape[0]
    k = to_m.shape[1]
    padded = recv_e.shape[0] - 2 * HW
    slots = far.shape[0] + near.shape[0]
    operands = (recv_e, recv_o, far, near, dens, cot, near_w, to_m, to_v, far_w)
    return pl.pallas_call(
        near_far_kernel,
        out_shape=[jax.ShapeDtypeStruct((rows, 128), F32)] * 2,
        in_specs=anywhere(10),
        out_specs=in_vmem(2),
        scratch_shapes=held(*operands)
        + [
            pltpu.VMEM((rows // TILE, TILE, 256), BF16),
            pltpu.VMEM((2 * HW, 256), BF16),
            pltpu.VMEM((padded, rows), F32),
            pltpu.VMEM((padded, 2 * HW), F32),
            pltpu.VMEM((rows, 128), F32),
            pltpu.VMEM((rows, slots * 128), BF16),
            pltpu.VMEM((rows, slots * 128), BF16),
            pltpu.VMEM((near.shape[0] * 128, 128), BF16),
            pltpu.VMEM((far.shape[0] * 128, k), BF16),
            pltpu.VMEM((far.shape[0] * 128, 128), BF16),
            pltpu.VMEM((far.shape[0] * 128, 128), BF16),
        ],
        compiler_params=pltpu.CompilerParams(vmem_limit_bytes=64 << 20),
        cost_estimate=pl.CostEstimate(flops=20 * 10**9, bytes_accessed=5 << 20, transcendentals=0),
        name="near_far",
    )(*operands)


def climb_call(dens, cot, far, near, to_m, to_v, merge, split, count, rim_shape):
    k = to_m.shape[1]
    chain = pltpu.VMEM((k // 128, dens.shape[0], 128), F32)
    operands = (dens, cot, far, near, to_m, to_v, merge, split)
    return pl.pallas_call(
        climb_kernel,
        out_shape=[
            jax.ShapeDtypeStruct((count * 8, 128), F32),
            rim_shape,
            rim_shape,
            jax.ShapeDtypeStruct((8, k, k), BF16),
        ],
        in_specs=anywhere(8),
        out_specs=in_vmem(4),
        scratch_shapes=held(*operands) + [chain, chain, pltpu.VMEM((k // 128, 8 * k, 128), F32)],
        compiler_params=pltpu.CompilerParams(vmem_limit_bytes=64 << 20),
        name="climb",
    )(*operands)


def fall_call(gathered, coarse_list, merge, split, far_w, to_m, to_v, near_pot, near_grad):
    rows = near_pot.shape[0]
    chain = pltpu.VMEM((merge.shape[2] // 128, rows, 128), F32)
    operands = (gathered, coarse_list, merge, split, far_w, to_m, to_v, near_pot, near_grad)
    return pl.pallas_call(
        fall_kernel,
        out_shape=[jax.ShapeDtypeStruct((rows, 128), F32)] * 2,
        in_specs=anywhere(9),
        out_specs=in_vmem(2),
        scratch_shapes=held(*operands) + [chain, chain],
        compiler_params=pltpu.CompilerParams(vmem_limit_bytes=64 << 20),
        name="fall",
    )(*operands)


def per_device(
    densities, cotangents, far_list, near_list, coarse_list,
    to_moments, merge_moments, far_translate, local_split, to_values, near_blocks,
):
    rows = densities.shape[0]
    k = to_moments.shape[1]
    count = lax.axis_size(AXES)
    slots = far_list.shape[0] + near_list.shape[0]
    rim_shape = jax.ShapeDtypeStruct((2 * HW + -(-slots // 16) * 16, 128), BF16)
    row, far_rim, near_rim, split = climb_call(
        densities, cotangents, far_list, near_list, to_moments, to_values, merge_moments, local_split,
        count, rim_shape,
    )
    pairs = [(i, i + 1) for i in range(1, count - 1, 2)]
    recv_o = lax.ppermute(far_rim, AXES, pairs + [(b, a) for a, b in pairs])
    recv_e = lax.ppermute(near_rim, AXES, [(i, i ^ 1) for i in range(count)])
    gathered = lax.all_to_all(row, AXES, 0, 0, tiled=True)
    sums = near_far_call(
        far_list, near_list, densities, cotangents, recv_e, recv_o,
        to_moments, to_values, far_translate, near_blocks,
    )
    return fall_call(
        gathered, coarse_list, merge_moments, split, far_translate, to_moments, to_values, *sums,
    )


def solution(mesh):
    rows = P(AXES, None)
    lists = P(None, AXES)
    return jax.shard_map(
        per_device,
        mesh=mesh,
        in_specs=(rows, rows, lists, lists) + (P(),) * 7,
        out_specs=(rows, rows),
        check_vma=False,
    )
```

time: 49.6 us -> 42.4 us (0.85)
  Pallas kernels: 31.9 us -> 24.2 us
    pallas_call x1, Pallas kernels: 18.6 us -> 13 us  [near_far_call(): pl.pallas_call(near_far_kernel, out_shape=[jax.ShapeDtypeStruct((rows, 12...]
    pallas_call x2, Pallas kernels: 13.3 us -> 11.2 us  [the longest x1 6.37 us: fall_call(): pl.pallas_call(fall_kernel, out_shape=[jax.ShapeDtypeStruct((rows, 128),...]
  transfers between devices with their start and end apart: 3 -> 3, of which waited for: 0 -> 1; matrix products, arithmetic and copies ran while one was open for 0% -> 0% of each run, Pallas kernels for 38% -> 31%
where the time goes in v2:
time: 42.4 us; the launch traced here: 42.2 us
  Pallas kernels  24.2 us (57%)
  starting transfers between devices  16.9 us (40%)
  between operations  0.84 us (2%)
    pallas_call x1, Pallas kernels, near_far_call(): pl.pallas_call(near_far_kernel, out_shape=[jax.ShapeDtypeStruct((rows, 12...  13 us
    ppermute x1, starting transfers between devices, per_device(): recv_o = lax.ppermute(far_rim, AXES, pairs + [(b, a) for a, b in pairs])  7.21 us
    all_to_all x1, starting transfers between devices, per_device(): gathered = lax.all_to_all(row, AXES, 0, 0, tiled=True)  7.11 us
    pallas_call x1, Pallas kernels, fall_call(): pl.pallas_call(fall_kernel, out_shape=[jax.ShapeDtypeStruct((rows, 128),...  6.37 us
    pallas_call x1, Pallas kernels, climb_call(): pl.pallas_call(climb_kernel, out_shape=[jax.ShapeDtypeStruct((count * 8,...  4.83 us
    ppermute x1, starting transfers between devices, per_device(): recv_e = lax.ppermute(near_rim, AXES, [(i, i ^ 1) for i in range(count)])  2.55 us
  transfers between devices with their start and end apart: 3, of which 1 were waited for; matrix products, arithmetic and copies ran while one was open for 0% of the time, Pallas kernels for 31%

profile of v2, /device:TPU:1, one launch (start us, length us, event | category | flops | bytes accessed | tf_op | source)
XLA Modules:
  0.0 42.2 jit_solution(5556881649378534989)
XLA Ops:
  0.6 4.8 %climb.1 = (f32[1024,128]{1,0:T(8,128)}, bf16[304,128]{1,0:T(8,128)(2,1)}, bf16[304,128]{1,0:T(8,128)(2,1)}, bf16[8,256,256]{2,1,0:T(8,128)(2,1)}) custom-call(bf16[512,128]{1,0:T(8,128)(2,1)} %refs_4_.4, bf16[512,128]{1,0:T(8,128)(2,1)} %refs_5_.4, s32[16,512]{1,0:T(8,128)} %refs_2_.4, s32[27,512]{1,0:T(8,128)} %refs_3_.3, bf16[128,256]{1,0:T(8,128)(2,1)} %refs_5_.5, ...), custom_call_target="tpu_custom_call" | custom-call | tf_op jit(solution)/shard_map/climb/pallas_call | solution.py:289
  5.5 2.5 %collective-permute-start = (bf16[304,128]{1,0:T(8,128)(2,1)}, bf16[304,128]{1,0:T(8,128)(2,1)}, u32[]{:S(2)}, u32[]{:S(2)}) collective-permute-start(bf16[304,128]{1,0:T(8,128)(2,1)} %get-tuple-element.10), channel_id=1, source_target_pairs={{0,1},{1,0},{2,3},{3,2},{4,5},{5,4},{6,7},{7,6},{8,9},{9,8},{10,11... | collective-permute-start | bytes 233480 | tf_op jit(solution)/shard_map/ppermute | solution.py:335
  8.0 7.2 %collective-permute-start.1 = (bf16[304,128]{1,0:T(8,128)(2,1)}, bf16[304,128]{1,0:T(8,128)(2,1)}, u32[]{:S(2)}, u32[]{:S(2)}) collective-permute-start(bf16[304,128]{1,0:T(8,128)(2,1)} %get-tuple-element.11), channel_id=1, source_target_pairs={{1,2},{3,4},{5,6},{7,8},{9,10},{11,12},{13,14},{15,16},{17,18},{19... | collective-permute-start | bytes 233480 | tf_op jit(solution)/shard_map/ppermute | solution.py:334
  15.2 7.1 %all-to-all-start = ((f32[128,8,128]{2,1,0:T(8,128)}), f32[128,8,128]{2,1,0:T(8,128)}, u32[]{:S(2)}, u32[]{:S(2)}) async-start(f32[128,8,128]{2,1,0:T(8,128)} %bitcast.2), calls=%async_computation | async-start | bytes 1048576 | tf_op jit(solution)/shard_map/all_to_all | solution.py:336
  22.4 0.0 collective-permute-done.refs_0_
  22.4 0.0 collective-permute-done.1.refs_1_
  22.4 13.0 %near_far.1 = (f32[512,128]{1,0:T(8,128)}, f32[512,128]{1,0:T(8,128)}) custom-call(bf16[304,128]{1,0:T(8,128)(2,1)} %collective-permute-done.refs_0_, bf16[304,128]{1,0:T(8,128)(2,1)} %collective-permute-done.1.refs_1_, s32[16,512]{1,0:T(8,128)} %refs_2_.4, s32[27,512]{1,0:T(8,128)} %refs_3_.3, bf16[512,128]{1,0:T(8,128)(2,1)} %refs_4_.4, ...), custom_call_target="tpu_custom_call" | custom-call | flops 20000000000 | bytes 5242880 | tf_op jit(solution)/shard_map/near_far/pallas_call | solution.py:260
  35.4 0.3 all-to-all-done
  35.7 6.4 %fall.1 = (f32[512,128]{1,0:T(8,128)}, f32[512,128]{1,0:T(8,128)}) custom-call(f32[1024,128]{1,0:T(8,128)} %bitcast.1.refs_0_, s32[16,16]{1,0:T(8,128)} %refs_1_.3, bf16[8,256,256]{2,1,0:T(8,128)(2,1)} %refs_2_.5, bf16[8,256,256]{2,1,0:T(8,128)(2,1)} %get-tuple-element.9.refs_3_, bf16[16,256,256]{2,1,0:T(8,128)(2,1)} %refs_4_.5, bf16[128,256]{1,0:T(8,128)(2,1)} %refs_5_.5, ...), custom_call_target="tpu_custom_call" | custom-call | tf_op jit(solution)/shard_map/fall/pallas_call | solution.py:309
Async XLA Ops:
  5.5 16.9 %collective-permute-start = (bf16[304,128]{1,0:T(8,128)(2,1)}, bf16[304,128]{1,0:T(8,128)(2,1)}, u32[]{:S(2)}, u32[]{:S(2)}) collective-permute-start(bf16[304,128]{1,0:T(8,128)(2,1)} %get-tuple-element.10), channel_id=1, source_target_pairs={{0,1},{1,0},{2,3},{3,2},{4,5},{5,4},{6,7},{7,6},{8,9},{9,8},{10,11... | collective-permute-start | bytes 233480 | tf_op jit(solution)/shard_map/ppermute | solution.py:335
  8.0 14.3 %collective-permute-start.1 = (bf16[304,128]{1,0:T(8,128)(2,1)}, bf16[304,128]{1,0:T(8,128)(2,1)}, u32[]{:S(2)}, u32[]{:S(2)}) collective-permute-start(bf16[304,128]{1,0:T(8,128)(2,1)} %get-tuple-element.11), channel_id=1, source_target_pairs={{1,2},{3,4},{5,6},{7,8},{9,10},{11,12},{13,14},{15,16},{17,18},{19... | collective-permute-start | bytes 233480 | tf_op jit(solution)/shard_map/ppermute | solution.py:334
  15.2 20.5 %all-to-all-start = ((f32[128,8,128]{2,1,0:T(8,128)}), f32[128,8,128]{2,1,0:T(8,128)}, u32[]{:S(2)}, u32[]{:S(2)}) async-start(f32[128,8,128]{2,1,0:T(8,128)} %bitcast.2), calls=%async_computation | async-start | bytes 1048576 | tf_op jit(solution)/shard_map/all_to_all | solution.py:336

commit v3 on v2

--- a/solution.py
+++ b/solution.py
@@ -9,7 +9,7 @@
 
 HW = 128
 TILE = 256
-PAIR = 8
+ROWS = 4
 AXES = ("coarse", "leaf")
 F32 = jnp.float32
 BF16 = jnp.bfloat16
@@ -77,18 +77,20 @@
 
 def climb_kernel(*refs):
     sources, (out, far_rim, near_rim, split_by_child), rest = refs[:8], refs[8:12], refs[12:]
-    dens, cot, far, near, to_m, to_v, merge, split, sems, mom, adj, wide = rest
+    dens, cot, to_m, to_v, merge, split, far, near, sems, mom, adj, wide = rest
     fetch = Fetch(sources, rest[:8], sems)
     rows = dens.shape[0]
     k = to_m.shape[1]
     odd = lax.rem(here(), 2) == 1
-    fetch.wait(0, 1, 2, 3)
+    child = lax.rem(here(), 8)
+    fetch.wait(0, 2)
+    put_rows(mom, pl.ds(0, rows), rounded(dot(dens[...], to_m[...])))
+    fetch.wait(1, 3)
+    put_rows(adj, pl.ds(0, rows), rounded(dot(cot[...], to_v[...], NT)))
+    fetch.wait(6, 7)
     rim(odd, dens, cot, far, near, far_rim)
     rim(jnp.logical_not(odd), dens, cot, far, near, near_rim)
     fetch.wait(4, 5)
-    put_rows(mom, pl.ds(0, rows), rounded(dot(dens[...], to_m[...])))
-    put_rows(adj, pl.ds(0, rows), rounded(dot(cot[...], to_v[...], NT)))
-    fetch.wait(6, 7)
     for h in range(2):
         wide[h] = split[:, :, h * 128 : (h + 1) * 128].astype(F32).reshape(8 * k, 128)
     for c in range(8):
@@ -97,19 +99,22 @@
         rows //= 8
         adj_up = jnp.zeros((rows, k), F32)
         children = [pl.ds(c, rows, stride=8) if rows > 1 else pl.ds(c, 1) for c in range(8)]
-        up = jnp.concatenate([get_rows(mom, child) for child in children], axis=1).astype(BF16)
+        up = jnp.concatenate([get_rows(mom, at) for at in children], axis=1).astype(BF16)
         up = dot(up, merge[...].reshape(8 * k, k))
-        for c, child in enumerate(children):
-            adj_up += dot(get_rows(adj, child).astype(BF16), split_by_child[c], NT)
+        for c, at in enumerate(children):
+            adj_up += dot(get_rows(adj, at).astype(BF16), split_by_child[c], NT)
         put_rows(mom, pl.ds(0, rows), rounded(up))
         put_rows(adj, pl.ds(0, rows), rounded(adj_up))
-    row = jnp.concatenate([mom[0, :1], mom[1, :1], adj[0, :1], adj[1, :1], jnp.zeros((4, 128), F32)], axis=0)
+    up = dot(up.astype(BF16), merge[child])
+    adj_up = dot(adj_up.astype(BF16), split_by_child[child], NT)
+    row = jnp.concatenate([x[:, h * 128 : (h + 1) * 128] for x in (up, adj_up) for h in range(2)], axis=0)
+    row = jnp.concatenate([row, row], axis=0)
     out[...] = jnp.broadcast_to(row[None], (out.shape[0] // 8, 8, 128)).reshape(out.shape)
 
 
 def near_far_kernel(*refs):
     sources, (potential, gradient), rest = refs[:10], refs[10:12], refs[12:]
-    recv_e, recv_o, far, near, dens, cot, near_w, to_m, to_v, far_w, sems = rest[:11]
+    far, near, recv_e, recv_o, dens, cot, near_w, to_m, to_v, far_w, sems = rest[:11]
     dens_pair, cot_rim, row_place, rim_place, col_targets, picked, collected = rest[11:18]
     near_wt, far_half, far_op, far_opt = rest[18:]
     fetch = Fetch(sources, rest[:10], sems)
@@ -118,7 +123,16 @@
     n_far, n_near = far.shape[0], near.shape[0]
     slots = n_far + n_near
     padded = row_place.shape[0]
-    fetch.wait(0, 1, 2, 3, 4, 5)
+    fetch.wait(0, 1)
+    listed = jnp.concatenate(
+        [far[...].astype(F32), near[...].astype(F32), jnp.full((128 - slots, rows), -1.0, F32)], axis=0
+    )
+    place = (lax.broadcasted_iota(jnp.int32, listed.shape, 1) % TILE).astype(F32)
+    listed = jnp.where(listed >= 0, listed + place, -1.0)
+    col_targets[...] = listed.T
+    listed = listed[:padded]
+    row_place[...] = jnp.where(listed >= TILE, listed - TILE, listed)
+    fetch.wait(2, 3, 4, 5)
     odd = lax.rem(here(), 2) == 1
     first, second = recv_e[...], recv_o[...]
     left = jnp.where(odd, first, second)
@@ -131,15 +145,6 @@
     cot_rim[...] = jnp.zeros(cot_rim.shape, BF16)
     cot_rim[:HW, :128] = left[HW : 2 * HW]
     cot_rim[HW:, 128:] = right[HW : 2 * HW]
-
-    listed = jnp.concatenate(
-        [far[...].astype(F32), near[...].astype(F32), jnp.full((128 - slots, rows), -1.0, F32)], axis=0
-    )
-    place = (lax.broadcasted_iota(jnp.int32, listed.shape, 1) % TILE).astype(F32)
-    listed = jnp.where(listed >= 0, listed + place, -1.0)
-    col_targets[...] = listed.T
-    listed = listed[:padded]
-    row_place[...] = jnp.where(listed >= TILE, listed - TILE, listed)
     listed = jnp.concatenate([left[2 * HW :].astype(F32), right[2 * HW :].astype(F32)], axis=1)
     lane = lax.broadcasted_iota(jnp.int32, listed.shape, 1)
     place = jnp.where(lane < HW, lane - TILE, lane - HW).astype(F32)
@@ -202,31 +207,25 @@
 
 def fall_kernel(*refs):
     sources, (potential, gradient), rest = refs[:9], refs[9:11], refs[11:]
-    gathered, coarse_list, merge, split, far_w, to_m, to_v, near_pot, near_grad, sems, fall, adj_fall = rest
+    gathered, coarse_list, far_w, merge, split, to_m, to_v, near_pot, near_grad, sems, fall, adj_fall = rest
     fetch = Fetch(sources, rest[:9], sems)
     k = merge.shape[2]
     slots, boxes = coarse_list.shape
     box, child = here() // 8, lax.rem(here(), 8)
-    fetch.wait(0, 1, 2)
-
-    def children(c, first):
-        at = [gathered[pl.ds(PAIR * c + first + i, boxes, stride=PAIR * 8), :] for i in range(2)]
-        return jnp.concatenate(at, axis=1).astype(BF16)
-
-    moments = jnp.concatenate([children(c, 0) for c in range(8)], axis=1)
-    coarse_m = dot(moments, merge[...].reshape(8 * k, k)).astype(BF16)
-    fetch.wait(3)
-    coarse_a = jnp.zeros((boxes, k), F32)
-    for c in range(8):
-        coarse_a += dot(children(c, 2), split[c], NT)
-    coarse_a = coarse_a.astype(BF16)
+    fetch.wait(0, 1)
+    sums = []
+    for i in range(ROWS):
+        parts = [gathered[pl.ds(ROWS * c + i, boxes, stride=ROWS * 8), :] for c in range(8)]
+        sums.append(functools.reduce(jnp.add, parts))
+    coarse_m = jnp.concatenate(sums[:2], axis=1).astype(BF16)
+    coarse_a = jnp.concatenate(sums[2:], axis=1).astype(BF16)
     listed = coarse_list[...]
     across = lax.broadcasted_iota(jnp.int32, listed.shape, 1)
     named = jnp.sum(jnp.where(across == box, listed, 0), axis=1, keepdims=True)
     picked = dot(jnp.where(across == named, 1.0, 0.0).astype(BF16), coarse_m)
     collected = dot(jnp.where(listed == box, 1.0, 0.0).astype(BF16), coarse_a).astype(BF16)
     picked = jnp.concatenate([picked[j : j + 1, :] for j in range(slots)], axis=1).astype(BF16)
-    fetch.wait(4)
+    fetch.wait(2)
     operators = far_w[...].reshape(slots * k, k)
     top = dot(picked, operators).astype(BF16)
     spread = dot(collected, operators, NT)
@@ -234,6 +233,7 @@
     for j in range(1, slots):
         adj_top += spread[j : j + 1, j * k : (j + 1) * k]
     adj_top = adj_top.astype(BF16)
+    fetch.wait(3, 4)
     put_rows(fall, pl.ds(0, 1), rounded(dot(top, split[child])))
     put_rows(adj_fall, pl.ds(0, 1), rounded(dot(adj_top, merge[child], NT)))
     rows = 1
@@ -256,7 +256,7 @@
     k = to_m.shape[1]
     padded = recv_e.shape[0] - 2 * HW
     slots = far.shape[0] + near.shape[0]
-    operands = (recv_e, recv_o, far, near, dens, cot, near_w, to_m, to_v, far_w)
+    operands = (far, near, recv_e, recv_o, dens, cot, near_w, to_m, to_v, far_w)
     return pl.pallas_call(
         near_far_kernel,
         out_shape=[jax.ShapeDtypeStruct((rows, 128), F32)] * 2,
@@ -285,11 +285,11 @@
 def climb_call(dens, cot, far, near, to_m, to_v, merge, split, count, rim_shape):
     k = to_m.shape[1]
     chain = pltpu.VMEM((k // 128, dens.shape[0], 128), F32)
-    operands = (dens, cot, far, near, to_m, to_v, merge, split)
+    operands = (dens, cot, to_m, to_v, merge, split, far, near)
     return pl.pallas_call(
         climb_kernel,
         out_shape=[
-            jax.ShapeDtypeStruct((count * 8, 128), F32),
+            jax.ShapeDtypeStruct((count * ROWS, 128), F32),
             rim_shape,
             rim_shape,
             jax.ShapeDtypeStruct((8, k, k), BF16),
@@ -305,7 +305,7 @@
 def fall_call(gathered, coarse_list, merge, split, far_w, to_m, to_v, near_pot, near_grad):
     rows = near_pot.shape[0]
     chain = pltpu.VMEM((merge.shape[2] // 128, rows, 128), F32)
-    operands = (gathered, coarse_list, merge, split, far_w, to_m, to_v, near_pot, near_grad)
+    operands = (gathered, coarse_list, far_w, merge, split, to_m, to_v, near_pot, near_grad)
     return pl.pallas_call(
         fall_kernel,
         out_shape=[jax.ShapeDtypeStruct((rows, 128), F32)] * 2,

time: 42.4 us -> 40.9 us (0.965)
  Pallas kernels: 24.2 us -> 23 us
    pallas_call x1, Pallas kernels: 6.37 us -> 5.44 us  [fall_call(): pl.pallas_call(fall_kernel, out_shape=[jax.ShapeDtypeStruct((rows, 128),...]
  transfers between devices with their start and end apart: 3 -> 3, of which waited for: 1 -> 0; matrix products, arithmetic and copies ran while one was open for 0% -> 0% of each run, Pallas kernels for 31% -> 31%
where the time goes in v3:
time: 40.9 us; the launch traced here: 40.8 us
  Pallas kernels  23 us (56%)
  starting transfers between devices  16.9 us (41%)
  between operations  0.85 us (2%)
    pallas_call x1, Pallas kernels, near_far_call(): pl.pallas_call(near_far_kernel, out_shape=[jax.ShapeDtypeStruct((rows, 12...  12.8 us
    ppermute x1, starting transfers between devices, per_device(): recv_o = lax.ppermute(far_rim, AXES, pairs + [(b, a) for a, b in pairs])  7.21 us
    all_to_all x1, starting transfers between devices, per_device(): gathered = lax.all_to_all(row, AXES, 0, 0, tiled=True)  7.11 us
    pallas_call x1, Pallas kernels, fall_call(): pl.pallas_call(fall_kernel, out_shape=[jax.ShapeDtypeStruct((rows, 128),...  5.44 us
    pallas_call x1, Pallas kernels, climb_call(): pl.pallas_call(climb_kernel, out_shape=[jax.ShapeDtypeStruct((count * ROW...  4.77 us
    ppermute x1, starting transfers between devices, per_device(): recv_e = lax.ppermute(near_rim, AXES, [(i, i ^ 1) for i in range(count)])  2.55 us
  transfers between devices with their start and end apart: 3, of which 0 were waited for; matrix products, arithmetic and copies ran while one was open for 0% of the time, Pallas kernels for 31%

profile of v3, /device:TPU:1, one launch (start us, length us, event | category | flops | bytes accessed | tf_op | source)
XLA Modules:
  0.0 40.8 jit_solution(8620682339242044968)
XLA Ops:
  0.6 4.8 %climb.1 = (f32[512,128]{1,0:T(8,128)}, bf16[304,128]{1,0:T(8,128)(2,1)}, bf16[304,128]{1,0:T(8,128)(2,1)}, bf16[8,256,256]{2,1,0:T(8,128)(2,1)}) custom-call(bf16[512,128]{1,0:T(8,128)(2,1)} %refs_4_.3, bf16[512,128]{1,0:T(8,128)(2,1)} %refs_5_.4, bf16[128,256]{1,0:T(8,128)(2,1)} %refs_5_.5, bf16[256,128]{1,0:T(8,128)(2,1)} %refs_6_.5, ...), custom_call_target="tpu_custom_call" | custom-call | tf_op jit(solution)/shard_map/climb/pallas_call | solution.py:289
  5.4 2.5 %collective-permute-start = (bf16[304,128]{1,0:T(8,128)(2,1)}, bf16[304,128]{1,0:T(8,128)(2,1)}, u32[]{:S(2)}, u32[]{:S(2)}) collective-permute-start(bf16[304,128]{1,0:T(8,128)(2,1)} %get-tuple-element.10), channel_id=1, source_target_pairs={{0,1},{1,0},{2,3},{3,2},{4,5},{5,4},{6,7},{7,6},{8,9},{9,8},{10,11... | collective-permute-start | bytes 233480 | tf_op jit(solution)/shard_map/ppermute | solution.py:335
  8.0 7.2 %collective-permute-start.1 = (bf16[304,128]{1,0:T(8,128)(2,1)}, bf16[304,128]{1,0:T(8,128)(2,1)}, u32[]{:S(2)}, u32[]{:S(2)}) collective-permute-start(bf16[304,128]{1,0:T(8,128)(2,1)} %get-tuple-element.11), channel_id=1, source_target_pairs={{1,2},{3,4},{5,6},{7,8},{9,10},{11,12},{13,14},{15,16},{17,18},{19... | collective-permute-start | bytes 233480 | tf_op jit(solution)/shard_map/ppermute | solution.py:334
  15.2 7.1 %all-to-all-start = ((f32[128,4,128]{2,1,0:T(4,128)}), f32[128,4,128]{2,1,0:T(4,128)}, u32[]{:S(2)}, u32[]{:S(2)}) async-start(f32[128,4,128]{2,1,0:T(4,128)} %bitcast.2), calls=%async_computation | async-start | bytes 524288 | tf_op jit(solution)/shard_map/all_to_all | solution.py:336
  22.3 0.0 collective-permute-done.refs_2_
  22.3 0.0 collective-permute-done.1.refs_3_
  22.3 12.8 %near_far.1 = (f32[512,128]{1,0:T(8,128)}, f32[512,128]{1,0:T(8,128)}) custom-call(s32[16,512]{1,0:T(8,128)} %refs_0_.3, s32[27,512]{1,0:T(8,128)} %refs_1_.4, bf16[304,128]{1,0:T(8,128)(2,1)} %collective-permute-done.refs_2_, bf16[304,128]{1,0:T(8,128)(2,1)} %collective-permute-done.1.refs_3_, bf16[512,128]{1,0:T(8,128)(2,1)} %refs_4_.3, ...), custom_call_target="tpu_custom_call" | custom-call | flops 20000000000 | bytes 5242880 | tf_op jit(solution)/shard_map/near_far/pallas_call | solution.py:260
  35.1 0.0 all-to-all-done
  35.1 5.4 %fall.1 = (f32[512,128]{1,0:T(8,128)}, f32[512,128]{1,0:T(8,128)}) custom-call(f32[512,128]{1,0:T(8,128)} %bitcast.1.refs_0_, s32[16,16]{1,0:T(8,128)} %refs_1_.5, bf16[16,256,256]{2,1,0:T(8,128)(2,1)} %refs_2_.3, bf16[8,256,256]{2,1,0:T(8,128)(2,1)} %refs_3_.3, bf16[8,256,256]{2,1,0:T(8,128)(2,1)} %get-tuple-element.9.refs_4_, bf16[128,256]{1,0:T(8,128)(2,1)} %refs_5_.5, ...), custom_call_target="tpu_custom_call" | custom-call | tf_op jit(solution)/shard_map/fall/pallas_call | solution.py:309
Async XLA Ops:
  5.4 16.9 %collective-permute-start = (bf16[304,128]{1,0:T(8,128)(2,1)}, bf16[304,128]{1,0:T(8,128)(2,1)}, u32[]{:S(2)}, u32[]{:S(2)}) collective-permute-start(bf16[304,128]{1,0:T(8,128)(2,1)} %get-tuple-element.10), channel_id=1, source_target_pairs={{0,1},{1,0},{2,3},{3,2},{4,5},{5,4},{6,7},{7,6},{8,9},{9,8},{10,11... | collective-permute-start | bytes 233480 | tf_op jit(solution)/shard_map/ppermute | solution.py:335
  8.0 14.3 %collective-permute-start.1 = (bf16[304,128]{1,0:T(8,128)(2,1)}, bf16[304,128]{1,0:T(8,128)(2,1)}, u32[]{:S(2)}, u32[]{:S(2)}) collective-permute-start(bf16[304,128]{1,0:T(8,128)(2,1)} %get-tuple-element.11), channel_id=1, source_target_pairs={{1,2},{3,4},{5,6},{7,8},{9,10},{11,12},{13,14},{15,16},{17,18},{19... | collective-permute-start | bytes 233480 | tf_op jit(solution)/shard_map/ppermute | solution.py:334
  15.2 20.0 %all-to-all-start = ((f32[128,4,128]{2,1,0:T(4,128)}), f32[128,4,128]{2,1,0:T(4,128)}, u32[]{:S(2)}, u32[]{:S(2)}) async-start(f32[128,4,128]{2,1,0:T(4,128)} %bitcast.2), calls=%async_computation | async-start | bytes 524288 | tf_op jit(solution)/shard_map/all_to_all | solution.py:336

commit v4 on v3

--- a/solution.py
+++ b/solution.py
@@ -114,10 +114,13 @@
 
 def near_far_kernel(*refs):
     sources, (potential, gradient), rest = refs[:10], refs[10:12], refs[12:]
-    far, near, recv_e, recv_o, dens, cot, near_w, to_m, to_v, far_w, sems = rest[:11]
+    far, near, recv_e, recv_o, dens, cot, op, to_m, to_v, far_w, sems = rest[:11]
     dens_pair, cot_rim, row_place, rim_place, col_targets, picked, collected = rest[11:18]
-    near_wt, far_half, far_op, far_opt = rest[18:]
-    fetch = Fetch(sources, rest[:10], sems)
+    far_half, opt = rest[18:]
+    first = far.shape[0]
+    targets = list(rest[:10])
+    targets[6] = near_w = op.at[pl.ds(first, near.shape[0])]
+    fetch = Fetch(sources, targets, sems)
     rows = dens.shape[0]
     blocks = rows // TILE
     n_far, n_near = far.shape[0], near.shape[0]
@@ -129,7 +132,8 @@
     )
     place = (lax.broadcasted_iota(jnp.int32, listed.shape, 1) % TILE).astype(F32)
     listed = jnp.where(listed >= 0, listed + place, -1.0)
-    col_targets[...] = listed.T
+    coded = jnp.where(listed >= TILE, TILE - 1 - listed, listed)
+    col_targets[...] = jnp.where(listed >= 0, coded, -1000.0).T
     listed = listed[:padded]
     row_place[...] = jnp.where(listed >= TILE, listed - TILE, listed)
     fetch.wait(2, 3, 4, 5)
@@ -163,12 +167,12 @@
             own = slice(p * TILE, (p + 1) * TILE)
             column = col_targets[own, :]
             column = jnp.take_along_axis(column, jnp.full(column.shape, slot, jnp.int32), axis=1)
-            upper = column >= TILE
-            place = jnp.where(upper, column - TILE, column).astype(BF16)
+            column = column.astype(BF16)
+            upper = column < zero
+            place = jnp.where(upper, -one - column, column)
             table = jnp.concatenate([jnp.where(c == place, one, zero) for c in lanes], axis=1)
-            both = dot(table, dens_pair[p])
-            picked[own, at] = jnp.where(upper, both[:, 128:], both[:, :128]).astype(BF16)
-            upper = column.astype(BF16) >= jnp.full((), TILE, BF16)
+            both = dot(table, dens_pair[p]).astype(BF16)
+            picked[own, at] = jnp.where(upper, both[:, 128:], both[:, :128])
             values = cot[own, :]
             halves = [jnp.where(upper, zero, values), jnp.where(upper, values, zero)]
             entry = jnp.broadcast_to(row_place[pl.ds(slot, 1), own], (TILE, TILE)).astype(BF16)
@@ -185,24 +189,22 @@
     def _(j):
         step(j)
 
-    fetch.wait(6)
+    fetch.wait(6, 7, 8, 9)
 
     @pl.loop(0, n_near, unroll=27)
     def _(j):
         step(j + n_far)
-        near_wt[pl.ds(pl.multiple_of(j * 128, 128), 128), :] = near_w[j].T
-
-    fetch.wait(7, 8, 9)
+        opt[pl.ds(pl.multiple_of((j + n_far) * 128, 128), 128), :] = op[j + n_far].T
+
     for j in range(n_far):
         far_half[j * 128 : (j + 1) * 128, :] = dot(to_m[...], far_w[j]).astype(BF16)
     operator = dot(far_half[...], to_v[...])
-    far_op[...] = operator.astype(BF16)
     for j in range(n_far):
-        far_opt[j * 128 : (j + 1) * 128, :] = operator[j * 128 : (j + 1) * 128].T.astype(BF16)
-    split = n_far * 128
-    near_op = near_w[...].reshape(near_wt.shape)
-    potential[...] = dot(picked[:, :split], far_op[...]) + dot(picked[:, split:], near_op)
-    gradient[...] = dot(collected[:, :split], far_opt[...]) + dot(collected[:, split:], near_wt[...])
+        part = operator[j * 128 : (j + 1) * 128]
+        op[j] = part.astype(BF16)
+        opt[j * 128 : (j + 1) * 128, :] = part.T.astype(BF16)
+    potential[...] = dot(picked[...], op[...].reshape(opt.shape))
+    gradient[...] = dot(collected[...], opt[...])
 
 
 def fall_kernel(*refs):
@@ -257,12 +259,14 @@
     padded = recv_e.shape[0] - 2 * HW
     slots = far.shape[0] + near.shape[0]
     operands = (far, near, recv_e, recv_o, dens, cot, near_w, to_m, to_v, far_w)
+    shapes = list(operands)
+    shapes[6] = jax.ShapeDtypeStruct((slots, 128, 128), BF16)
     return pl.pallas_call(
         near_far_kernel,
         out_shape=[jax.ShapeDtypeStruct((rows, 128), F32)] * 2,
         in_specs=anywhere(10),
         out_specs=in_vmem(2),
-        scratch_shapes=held(*operands)
+        scratch_shapes=held(*shapes)
         + [
             pltpu.VMEM((rows // TILE, TILE, 256), BF16),
             pltpu.VMEM((2 * HW, 256), BF16),
@@ -271,10 +275,8 @@
             pltpu.VMEM((rows, 128), F32),
             pltpu.VMEM((rows, slots * 128), BF16),
             pltpu.VMEM((rows, slots * 128), BF16),
-            pltpu.VMEM((near.shape[0] * 128, 128), BF16),
             pltpu.VMEM((far.shape[0] * 128, k), BF16),
-            pltpu.VMEM((far.shape[0] * 128, 128), BF16),
-            pltpu.VMEM((far.shape[0] * 128, 128), BF16),
+            pltpu.VMEM((slots * 128, 128), BF16),
         ],
         compiler_params=pltpu.CompilerParams(vmem_limit_bytes=64 << 20),
         cost_estimate=pl.CostEstimate(flops=20 * 10**9, bytes_accessed=5 << 20, transcendentals=0),

time: 40.9 us -> 40.7 us (level)
  no operation moved by 1% of the time
where the time goes in v4:
time: 40.7 us; the launch traced here: 40.5 us
  Pallas kernels  22.8 us (56%)
  starting transfers between devices  16.9 us (42%)
  between operations  0.85 us (2%)
    pallas_call x1, Pallas kernels, near_far_call(): pl.pallas_call(near_far_kernel, out_shape=[jax.ShapeDtypeStruct((rows, 12...  12.6 us
    ppermute x1, starting transfers between devices, per_device(): recv_o = lax.ppermute(far_rim, AXES, pairs + [(b, a) for a, b in pairs])  7.21 us
    all_to_all x1, starting transfers between devices, per_device(): gathered = lax.all_to_all(row, AXES, 0, 0, tiled=True)  7.11 us
    pallas_call x1, Pallas kernels, fall_call(): pl.pallas_call(fall_kernel, out_shape=[jax.ShapeDtypeStruct((rows, 128),...  5.44 us
    pallas_call x1, Pallas kernels, climb_call(): pl.pallas_call(climb_kernel, out_shape=[jax.ShapeDtypeStruct((count * ROW...  4.77 us
    ppermute x1, starting transfers between devices, per_device(): recv_e = lax.ppermute(near_rim, AXES, [(i, i ^ 1) for i in range(count)])  2.55 us
  transfers between devices with their start and end apart: 3, of which 0 were waited for; matrix products, arithmetic and copies ran while one was open for 0% of the time, Pallas kernels for 31%

profile of v4, /device:TPU:1, one launch (start us, length us, event | category | flops | bytes accessed | tf_op | source)
XLA Modules:
  0.0 40.5 jit_solution(16733990864941377012)
XLA Ops:
  0.6 4.8 %climb.1 = (f32[512,128]{1,0:T(8,128)}, bf16[304,128]{1,0:T(8,128)(2,1)}, bf16[304,128]{1,0:T(8,128)(2,1)}, bf16[8,256,256]{2,1,0:T(8,128)(2,1)}) custom-call(bf16[512,128]{1,0:T(8,128)(2,1)} %refs_4_.3, bf16[512,128]{1,0:T(8,128)(2,1)} %refs_5_.4, bf16[128,256]{1,0:T(8,128)(2,1)} %refs_5_.5, bf16[256,128]{1,0:T(8,128)(2,1)} %refs_6_.5, ...), custom_call_target="tpu_custom_call" | custom-call | tf_op jit(solution)/shard_map/climb/pallas_call | solution.py:291
  5.4 2.5 %collective-permute-start = (bf16[304,128]{1,0:T(8,128)(2,1)}, bf16[304,128]{1,0:T(8,128)(2,1)}, u32[]{:S(2)}, u32[]{:S(2)}) collective-permute-start(bf16[304,128]{1,0:T(8,128)(2,1)} %get-tuple-element.10), channel_id=1, source_target_pairs={{0,1},{1,0},{2,3},{3,2},{4,5},{5,4},{6,7},{7,6},{8,9},{9,8},{10,11... | collective-permute-start | bytes 233480 | tf_op jit(solution)/shard_map/ppermute | solution.py:337
  8.0 7.2 %collective-permute-start.1 = (bf16[304,128]{1,0:T(8,128)(2,1)}, bf16[304,128]{1,0:T(8,128)(2,1)}, u32[]{:S(2)}, u32[]{:S(2)}) collective-permute-start(bf16[304,128]{1,0:T(8,128)(2,1)} %get-tuple-element.11), channel_id=1, source_target_pairs={{1,2},{3,4},{5,6},{7,8},{9,10},{11,12},{13,14},{15,16},{17,18},{19... | collective-permute-start | bytes 233480 | tf_op jit(solution)/shard_map/ppermute | solution.py:336
  15.2 7.1 %all-to-all-start = ((f32[128,4,128]{2,1,0:T(4,128)}), f32[128,4,128]{2,1,0:T(4,128)}, u32[]{:S(2)}, u32[]{:S(2)}) async-start(f32[128,4,128]{2,1,0:T(4,128)} %bitcast.2), calls=%async_computation | async-start | bytes 524288 | tf_op jit(solution)/shard_map/all_to_all | solution.py:338
  22.3 0.0 collective-permute-done.refs_2_
  22.3 0.0 collective-permute-done.1.refs_3_
  22.3 12.6 %near_far.1 = (f32[512,128]{1,0:T(8,128)}, f32[512,128]{1,0:T(8,128)}) custom-call(s32[16,512]{1,0:T(8,128)} %refs_0_.3, s32[27,512]{1,0:T(8,128)} %refs_1_.4, bf16[304,128]{1,0:T(8,128)(2,1)} %collective-permute-done.refs_2_, bf16[304,128]{1,0:T(8,128)(2,1)} %collective-permute-done.1.refs_3_, bf16[512,128]{1,0:T(8,128)(2,1)} %refs_4_.3, ...), custom_call_target="tpu_custom_call" | custom-call | flops 20000000000 | bytes 5242880 | tf_op jit(solution)/shard_map/near_far/pallas_call | solution.py:264
  34.9 0.0 all-to-all-done
  34.9 5.4 %fall.1 = (f32[512,128]{1,0:T(8,128)}, f32[512,128]{1,0:T(8,128)}) custom-call(f32[512,128]{1,0:T(8,128)} %bitcast.1.refs_0_, s32[16,16]{1,0:T(8,128)} %refs_1_.5, bf16[16,256,256]{2,1,0:T(8,128)(2,1)} %refs_2_.3, bf16[8,256,256]{2,1,0:T(8,128)(2,1)} %refs_3_.3, bf16[8,256,256]{2,1,0:T(8,128)(2,1)} %get-tuple-element.9.refs_4_, bf16[128,256]{1,0:T(8,128)(2,1)} %refs_5_.5, ...), custom_call_target="tpu_custom_call" | custom-call | tf_op jit(solution)/shard_map/fall/pallas_call | solution.py:311
Async XLA Ops:
  5.4 16.9 %collective-permute-start = (bf16[304,128]{1,0:T(8,128)(2,1)}, bf16[304,128]{1,0:T(8,128)(2,1)}, u32[]{:S(2)}, u32[]{:S(2)}) collective-permute-start(bf16[304,128]{1,0:T(8,128)(2,1)} %get-tuple-element.10), channel_id=1, source_target_pairs={{0,1},{1,0},{2,3},{3,2},{4,5},{5,4},{6,7},{7,6},{8,9},{9,8},{10,11... | collective-permute-start | bytes 233480 | tf_op jit(solution)/shard_map/ppermute | solution.py:337
  8.0 14.3 %collective-permute-start.1 = (bf16[304,128]{1,0:T(8,128)(2,1)}, bf16[304,128]{1,0:T(8,128)(2,1)}, u32[]{:S(2)}, u32[]{:S(2)}) collective-permute-start(bf16[304,128]{1,0:T(8,128)(2,1)} %get-tuple-element.11), channel_id=1, source_target_pairs={{1,2},{3,4},{5,6},{7,8},{9,10},{11,12},{13,14},{15,16},{17,18},{19... | collective-permute-start | bytes 233480 | tf_op jit(solution)/shard_map/ppermute | solution.py:336
  15.2 19.8 %all-to-all-start = ((f32[128,4,128]{2,1,0:T(4,128)}), f32[128,4,128]{2,1,0:T(4,128)}, u32[]{:S(2)}, u32[]{:S(2)}) async-start(f32[128,4,128]{2,1,0:T(4,128)} %bitcast.2), calls=%async_computation | async-start | bytes 524288 | tf_op jit(solution)/shard_map/all_to_all | solution.py:338

commit v5 on v4

--- a/solution.py
+++ b/solution.py
@@ -38,12 +38,12 @@
 
 
 class Fetch:
-    def __init__(self, sources, targets, sems):
+    def __init__(self, sources, targets, sems, order=None):
         self.copies = [
             pltpu.make_async_copy(s, t, sems.at[i]) for i, (s, t) in enumerate(zip(sources, targets))
         ]
-        for copy in self.copies:
-            copy.start()
+        for i in order or range(len(self.copies)):
+            self.copies[i].start()
 
     def wait(self, *which):
         for i in which:
@@ -210,7 +210,12 @@
 def fall_kernel(*refs):
     sources, (potential, gradient), rest = refs[:9], refs[9:11], refs[11:]
     gathered, coarse_list, far_w, merge, split, to_m, to_v, near_pot, near_grad, sems, fall, adj_fall = rest
-    fetch = Fetch(sources, rest[:9], sems)
+    half = far_w.shape[0] // 2
+    sources, targets = list(sources), list(rest[:9])
+    for held_by in (sources, targets):
+        held_by.append(held_by[2].at[pl.ds(half, half)])
+        held_by[2] = held_by[2].at[pl.ds(0, half)]
+    fetch = Fetch(sources, targets, sems, (0, 1, 2, 9, 3, 4, 5, 6, 7, 8))
     k = merge.shape[2]
     slots, boxes = coarse_list.shape
     box, child = here() // 8, lax.rem(here(), 8)
@@ -227,13 +232,16 @@
     picked = dot(jnp.where(across == named, 1.0, 0.0).astype(BF16), coarse_m)
     collected = dot(jnp.where(listed == box, 1.0, 0.0).astype(BF16), coarse_a).astype(BF16)
     picked = jnp.concatenate([picked[j : j + 1, :] for j in range(slots)], axis=1).astype(BF16)
-    fetch.wait(2)
-    operators = far_w[...].reshape(slots * k, k)
-    top = dot(picked, operators).astype(BF16)
-    spread = dot(collected, operators, NT)
-    adj_top = spread[:1, :k]
-    for j in range(1, slots):
-        adj_top += spread[j : j + 1, j * k : (j + 1) * k]
+    half = slots // 2
+    top, adj_top = jnp.zeros((1, k), F32), jnp.zeros((1, k), F32)
+    for part, lo in enumerate((0, half)):
+        fetch.wait((2, 9)[part])
+        operators = far_w[lo : lo + half].reshape(half * k, k)
+        top += dot(picked[:, lo * k : (lo + half) * k], operators)
+        spread = dot(collected, operators, NT)
+        for j in range(half):
+            adj_top += spread[lo + j : lo + j + 1, j * k : (j + 1) * k]
+    top = top.astype(BF16)
     adj_top = adj_top.astype(BF16)
     fetch.wait(3, 4)
     put_rows(fall, pl.ds(0, 1), rounded(dot(top, split[child])))
@@ -313,7 +321,7 @@
         out_shape=[jax.ShapeDtypeStruct((rows, 128), F32)] * 2,
         in_specs=anywhere(9),
         out_specs=in_vmem(2),
-        scratch_shapes=held(*operands) + [chain, chain],
+        scratch_shapes=held(*operands)[:-1] + [pltpu.SemaphoreType.DMA((10,)), chain, chain],
         compiler_params=pltpu.CompilerParams(vmem_limit_bytes=64 << 20),
         name="fall",
     )(*operands)

time: 40.7 us -> 40.5 us (level)
  no operation moved by 1% of the time
where the time goes in v5:
time: 40.5 us; the launch traced here: 40.3 us
  Pallas kernels  22.6 us (56%)
  starting transfers between devices  16.9 us (42%)
  between operations  0.85 us (2%)
    pallas_call x1, Pallas kernels, near_far_call(): pl.pallas_call(near_far_kernel, out_shape=[jax.ShapeDtypeStruct((rows, 12...  12.6 us
    ppermute x1, starting transfers between devices, per_device(): recv_o = lax.ppermute(far_rim, AXES, pairs + [(b, a) for a, b in pairs])  7.21 us
    all_to_all x1, starting transfers between devices, per_device(): gathered = lax.all_to_all(row, AXES, 0, 0, tiled=True)  7.11 us
    pallas_call x1, Pallas kernels, fall_call(): pl.pallas_call(fall_kernel, out_shape=[jax.ShapeDtypeStruct((rows, 128),...  5.19 us
    pallas_call x1, Pallas kernels, climb_call(): pl.pallas_call(climb_kernel, out_shape=[jax.ShapeDtypeStruct((count * ROW...  4.77 us
    ppermute x1, starting transfers between devices, per_device(): recv_e = lax.ppermute(near_rim, AXES, [(i, i ^ 1) for i in range(count)])  2.55 us
  transfers between devices with their start and end apart: 3, of which 0 were waited for; matrix products, arithmetic and copies ran while one was open for 0% of the time, Pallas kernels for 31%

profile of v5, /device:TPU:1, one launch (start us, length us, event | category | flops | bytes accessed | tf_op | source)
XLA Modules:
  0.0 40.3 jit_solution(15703177795682519121)
XLA Ops:
  0.6 4.8 %climb.1 = (f32[512,128]{1,0:T(8,128)}, bf16[304,128]{1,0:T(8,128)(2,1)}, bf16[304,128]{1,0:T(8,128)(2,1)}, bf16[8,256,256]{2,1,0:T(8,128)(2,1)}) custom-call(bf16[512,128]{1,0:T(8,128)(2,1)} %refs_4_.3, bf16[512,128]{1,0:T(8,128)(2,1)} %refs_5_.4, bf16[128,256]{1,0:T(8,128)(2,1)} %refs_5_.5, bf16[256,128]{1,0:T(8,128)(2,1)} %refs_6_.5, ...), custom_call_target="tpu_custom_call" | custom-call | tf_op jit(solution)/shard_map/climb/pallas_call | solution.py:299
  5.4 2.5 %collective-permute-start = (bf16[304,128]{1,0:T(8,128)(2,1)}, bf16[304,128]{1,0:T(8,128)(2,1)}, u32[]{:S(2)}, u32[]{:S(2)}) collective-permute-start(bf16[304,128]{1,0:T(8,128)(2,1)} %get-tuple-element.10), channel_id=1, source_target_pairs={{0,1},{1,0},{2,3},{3,2},{4,5},{5,4},{6,7},{7,6},{8,9},{9,8},{10,11... | collective-permute-start | bytes 233480 | tf_op jit(solution)/shard_map/ppermute | solution.py:345
  8.0 7.2 %collective-permute-start.1 = (bf16[304,128]{1,0:T(8,128)(2,1)}, bf16[304,128]{1,0:T(8,128)(2,1)}, u32[]{:S(2)}, u32[]{:S(2)}) collective-permute-start(bf16[304,128]{1,0:T(8,128)(2,1)} %get-tuple-element.11), channel_id=1, source_target_pairs={{1,2},{3,4},{5,6},{7,8},{9,10},{11,12},{13,14},{15,16},{17,18},{19... | collective-permute-start | bytes 233480 | tf_op jit(solution)/shard_map/ppermute | solution.py:344
  15.2 7.1 %all-to-all-start = ((f32[128,4,128]{2,1,0:T(4,128)}), f32[128,4,128]{2,1,0:T(4,128)}, u32[]{:S(2)}, u32[]{:S(2)}) async-start(f32[128,4,128]{2,1,0:T(4,128)} %bitcast.2), calls=%async_computation | async-start | bytes 524288 | tf_op jit(solution)/shard_map/all_to_all | solution.py:346
  22.3 0.0 collective-permute-done.refs_2_
  22.3 0.0 collective-permute-done.1.refs_3_
  22.3 12.6 %near_far.1 = (f32[512,128]{1,0:T(8,128)}, f32[512,128]{1,0:T(8,128)}) custom-call(s32[16,512]{1,0:T(8,128)} %refs_0_.3, s32[27,512]{1,0:T(8,128)} %refs_1_.4, bf16[304,128]{1,0:T(8,128)(2,1)} %collective-permute-done.refs_2_, bf16[304,128]{1,0:T(8,128)(2,1)} %collective-permute-done.1.refs_3_, bf16[512,128]{1,0:T(8,128)(2,1)} %refs_4_.3, ...), custom_call_target="tpu_custom_call" | custom-call | flops 20000000000 | bytes 5242880 | tf_op jit(solution)/shard_map/near_far/pallas_call | solution.py:272
  34.9 0.0 all-to-all-done
  34.9 5.2 %fall.1 = (f32[512,128]{1,0:T(8,128)}, f32[512,128]{1,0:T(8,128)}) custom-call(f32[512,128]{1,0:T(8,128)} %bitcast.1.refs_0_, s32[16,16]{1,0:T(8,128)} %refs_1_.5, bf16[16,256,256]{2,1,0:T(8,128)(2,1)} %refs_2_.3, bf16[8,256,256]{2,1,0:T(8,128)(2,1)} %refs_3_.3, bf16[8,256,256]{2,1,0:T(8,128)(2,1)} %get-tuple-element.9.refs_4_, bf16[128,256]{1,0:T(8,128)(2,1)} %refs_5_.5, ...), custom_call_target="tpu_custom_call" | custom-call | tf_op jit(solution)/shard_map/fall/pallas_call | solution.py:319
Async XLA Ops:
  5.4 16.9 %collective-permute-start = (bf16[304,128]{1,0:T(8,128)(2,1)}, bf16[304,128]{1,0:T(8,128)(2,1)}, u32[]{:S(2)}, u32[]{:S(2)}) collective-permute-start(bf16[304,128]{1,0:T(8,128)(2,1)} %get-tuple-element.10), channel_id=1, source_target_pairs={{0,1},{1,0},{2,3},{3,2},{4,5},{5,4},{6,7},{7,6},{8,9},{9,8},{10,11... | collective-permute-start | bytes 233480 | tf_op jit(solution)/shard_map/ppermute | solution.py:345
  8.0 14.3 %collective-permute-start.1 = (bf16[304,128]{1,0:T(8,128)(2,1)}, bf16[304,128]{1,0:T(8,128)(2,1)}, u32[]{:S(2)}, u32[]{:S(2)}) collective-permute-start(bf16[304,128]{1,0:T(8,128)(2,1)} %get-tuple-element.11), channel_id=1, source_target_pairs={{1,2},{3,4},{5,6},{7,8},{9,10},{11,12},{13,14},{15,16},{17,18},{19... | collective-permute-start | bytes 233480 | tf_op jit(solution)/shard_map/ppermute | solution.py:344
  15.2 19.8 %all-to-all-start = ((f32[128,4,128]{2,1,0:T(4,128)}), f32[128,4,128]{2,1,0:T(4,128)}, u32[]{:S(2)}, u32[]{:S(2)}) async-start(f32[128,4,128]{2,1,0:T(4,128)} %bitcast.2), calls=%async_computation | async-start | bytes 524288 | tf_op jit(solution)/shard_map/all_to_all | solution.py:346
